TPU v7x, 128 devices: a whole 4x4x4 slice. The times are simulated.
128 devices in a mesh: row: 8 (over y_lo, x), head: 16 (over y_hi, z, core).
Axes of the slice: x: 4, y: 4 (y_hi: 2, y_lo: 2; y = y_hi * 2 + y_lo), z: 4, core: 2. Of those that a mesh axis runs over, the one named last changes fastest.
Arguments:
- link_tensor_source: bfloat16 [128, 256, 256], P('head', 'row'), may hold values from -6 to 6
- neighbour_allowance: int32 [256, 256], P('row'), may hold values 0 or 1
- asking_projector: bfloat16 [128, 128], P(None, 'head'), may hold values from -0.5 to 0.5
- lookup_projector: bfloat16 [128, 128], P(None, 'head'), may hold values from -0.5 to 0.5
- first_content_projector: bfloat16 [128, 128], P(None, 'head'), may hold values from -0.5 to 0.5
- second_content_projector: bfloat16 [128, 128], P(None, 'head'), may hold values from -0.5 to 0.5
- final_projector: bfloat16 [128, 128], P('head'), may hold values from -0.5 to 0.5
- per_slot_scaling: float32 [16], P('head'), may hold values from 0.15 to 2, as said below
- upstream_sensitivity: bfloat16 [128, 256, 256], P('head', 'row'), may hold values from -48 to 48
Outputs:
- grad_pairs: bfloat16 [128, 256, 256], P('head', 'row')
- grad_query: float32 [128, 128], P(None, 'head')
- grad_key: float32 [128, 128], P(None, 'head')
- grad_left: float32 [128, 128], P(None, 'head')
- grad_right: float32 [128, 128], P(None, 'head')
- grad_out: float32 [128, 128], P('head')
Inputs may be any that keep to these rules, and one draw needn't show every extreme that they name: `per_slot_scaling`: 16 positive factors, one a head.
All inputs are finite; a program needn't handle non-finite values. No bound on the sum of `neighbour_allowance` on one device may be relied on, other than what follows from the above.
Results may differ from a plain program's by a relative error of at most 0.0025.
The roundings to bfloat16 on the way count: a program that leaves them out, or rounds other values in their place, can miss the bound.
Values may be sent and summed in bfloat16 or wider, within the bound.
A program may use at most 64 MiB of HBM per device.

v0:
```python
import jax
import jax.numpy as jnp
from jax import lax
from jax.sharding import PartitionSpec as P

HIGH = lax.Precision.HIGHEST
NEG = -1e30


def head_grads(query, key_all, left, right_all, stacked_derivative, factor, valid, keys_wanted):
    chans, rows, width = query.shape
    panel = min(32, width)
    blocks = width // panel
    grad_wide = stacked_derivative.astype(jnp.float32)

    def scores(number):
        begin = number * panel
        query_block = lax.dynamic_slice_in_dim(query, begin, panel, 2).astype(jnp.float32)
        key_block = lax.dynamic_slice_in_dim(key_all, begin, panel, 1).astype(jnp.float32)
        left_block = lax.dynamic_slice_in_dim(left, begin, panel, 2).astype(jnp.float32)
        right_block = lax.dynamic_slice_in_dim(right_all, begin, panel, 1).astype(jnp.float32)
        allowed = lax.dynamic_slice_in_dim(valid, begin, panel, 1)
        raw = jnp.einsum("cil,clj->ilj", query_block, key_block, precision=HIGH)
        logits = jnp.where(allowed[:, :, None], factor * raw, NEG)
        return (logits, allowed, query_block, key_block, left_block, right_block)

    def forward(state, number):
        top, total, accum = state
        logits, allowed, query_block, key_block, left_block, right_block = scores(number)
        new_top = jnp.maximum(top, logits.max(axis=1))
        keep = jnp.exp(top - new_top)
        weights = jnp.exp(logits - new_top[:, None, :])
        total = total * keep + weights.sum(axis=1)
        accum = accum * keep[None] + (
            weights[None] * left_block[:, :, :, None] * right_block[:, None, :, :]
        ).sum(axis=2)
        return ((new_top, total, accum), None)

    start_state = (
        jnp.full((rows, width), NEG, jnp.float32),
        jnp.zeros((rows, width), jnp.float32),
        jnp.zeros((chans, rows, width), jnp.float32),
    )
    (top, total, accum), _ = lax.scan(forward, start_state, jnp.arange(blocks))
    mixed = accum / total[None]
    delta = (grad_wide * mixed).sum(axis=0)

    def backward(state, number):
        logits, allowed, query_block, key_block, left_block, right_block = scores(number)
        prob = jnp.where(
            allowed[:, :, None], jnp.exp(logits - top[:, None, :]) / total[:, None, :], 0.0
        )
        grad_prob = (
            grad_wide[:, :, None, :] * left_block[:, :, :, None] * right_block[:, None, :, :]
        ).sum(axis=0)
        grad_score = prob * (grad_prob - delta[:, None, :])
        query_grad = factor * jnp.einsum("ilj,clj->cil", grad_score, key_block, precision=HIGH)
        left_grad = (prob[None] * grad_wide[:, :, None, :] * right_block[:, None, :, :]).sum(axis=3)
        key_grad = factor * jnp.einsum("ilj,cil->clj", grad_score, query_block, precision=HIGH)
        right_grad = (prob[None] * grad_wide[:, :, None, :] * left_block[:, :, :, None]).sum(axis=1)
        return (state, (query_grad, left_grad, key_grad, right_grad))

    _, outputs = lax.scan(backward, None, jnp.arange(blocks))
    query_grads = jnp.moveaxis(outputs[0], 0, 2).reshape(chans, rows, width)
    left_grads = jnp.moveaxis(outputs[1], 0, 2).reshape(chans, rows, width)
    stats = (top, total, delta)
    key_grads = jnp.moveaxis(outputs[2], 0, 1).reshape(chans, width, width)
    right_grads = jnp.moveaxis(outputs[3], 0, 1).reshape(chans, width, width)
    return (
        mixed.astype(jnp.bfloat16),
        query_grads.astype(jnp.bfloat16),
        left_grads.astype(jnp.bfloat16),
        key_grads,
        right_grads,
    ) + stats


def local(
    link_tensor_source,
    neighbour_allowance,
    asking_projector,
    lookup_projector,
    first_content_projector,
    second_content_projector,
    final_projector,
    per_slot_scaling,
    upstream_sensitivity,
):
    chans, rows, width = link_tensor_source.shape
    model = asking_projector.shape[0]
    resident_attention_slots = per_slot_scaling.shape[0]
    head_width = chans // resident_attention_slots
    inverse = 1.0 / width
    w_cat = jnp.concatenate(
        [asking_projector, lookup_projector, first_content_projector, second_content_projector],
        axis=1,
    )
    whole_pairs, whole_cot = (
        lax.all_gather(link_tensor_source, "head", axis=0, tiled=True),
        lax.all_gather(upstream_sensitivity, "head", axis=0, tiled=True),
    )
    flat_pairs = whole_pairs.reshape(model, rows * width)
    flat_cot = whole_cot.reshape(model, rows * width)
    mapped_activations = lax.dot_general(
        w_cat, flat_pairs, (((0,), (0,)), ((), ())), preferred_element_type=jnp.float32
    )
    stacked_derivative = jnp.dot(final_projector, flat_cot, preferred_element_type=jnp.float32)
    mapped_activations = mapped_activations.astype(jnp.bfloat16).reshape(4, chans, rows, width)
    query_part = mapped_activations[0]
    key_part = mapped_activations[1]
    left_part = mapped_activations[2]
    right_part = mapped_activations[3]
    stacked_derivative = stacked_derivative.astype(jnp.bfloat16).reshape(chans, rows, width)
    key_all, right_all = (
        lax.all_gather(key_part, "row", axis=1, tiled=True),
        lax.all_gather(right_part, "row", axis=1, tiled=True),
    )
    first_row = lax.axis_index("row") * rows
    columns = jnp.arange(width, dtype=jnp.int32)
    own_node = (first_row + jnp.arange(rows, dtype=jnp.int32))[:, None] == columns[None, :]
    valid = (neighbour_allowance == 1) | own_node

    def split_heads(array):
        return array.reshape((resident_attention_slots, head_width) + array.shape[1:])

    heads_in = (
        split_heads(query_part),
        split_heads(key_all),
        split_heads(left_part),
        split_heads(right_all),
        split_heads(stacked_derivative),
        per_slot_scaling,
    )
    mixed, back_query, back_left, key_terms, right_terms, top, total, delta = lax.map(
        lambda group: head_grads(*group, valid, True), heads_in
    )
    key_sum, right_sum = (
        lax.psum_scatter(
            key_terms.reshape(chans, width, width), "row", scatter_dimension=1, tiled=True
        ),
        lax.psum_scatter(
            right_terms.reshape(chans, width, width), "row", scatter_dimension=1, tiled=True
        ),
    )
    back_key = key_sum.astype(jnp.bfloat16)
    back_right = right_sum.astype(jnp.bfloat16)
    mixed = mixed.reshape(chans, rows * width)
    back_query = back_query.reshape(chans, rows, width)
    back_left = back_left.reshape(chans, rows, width)
    backs = jnp.concatenate([back_query, back_key, back_left, back_right], axis=0)
    backs_flat = backs.reshape(4 * chans, rows * width)
    all_columns = lax.all_gather(w_cat, "head", axis=1, tiled=True)
    own_rows = lax.dynamic_slice_in_dim(all_columns, lax.axis_index("head") * chans, chans, 0)
    piece = lax.all_gather(backs, "head", axis=0, tiled=True)
    amount = piece.shape[0]
    grad_flat = jnp.dot(
        own_rows, piece.reshape(amount, rows * width), preferred_element_type=jnp.float32
    )
    grad_pairs = grad_flat.astype(jnp.bfloat16).reshape(chans, rows, width)
    partial_weights = lax.dot_general(
        flat_pairs, backs_flat, (((1,), (1,)), ((), ())), preferred_element_type=jnp.float32
    )
    partial_out = lax.dot_general(
        mixed, flat_cot, (((1,), (1,)), ((), ())), preferred_element_type=jnp.float32
    )
    grad_weights, grad_out = lax.psum((partial_weights * inverse, partial_out * inverse), "row")
    return (
        grad_pairs,
        grad_weights[:, 0:chans],
        grad_weights[:, chans : 2 * chans],
        grad_weights[:, 2 * chans : 3 * chans],
        grad_weights[:, 3 * chans : 4 * chans],
        grad_out,
    )


def solution(mesh):
    placed = (
        P("head", "row", None),
        P("row", None),
        P(None, "head"),
        P(None, "head"),
        P(None, "head"),
        P(None, "head"),
        P("head", None),
        P("head"),
        P("head", "row", None),
    )
    return jax.shard_map(
        local,
        mesh=mesh,
        in_specs=placed,
        out_specs=(
            P("head", "row", None),
            P(None, "head"),
            P(None, "head"),
            P(None, "head"),
            P(None, "head"),
            P("head", None),
        ),
        check_vma=False,
    )
```

profile of v0, /device:TPU:1, one launch (start us, length us, event | category | flops | bytes accessed | tf_op | source)
XLA Modules:
  0.0 560.0 jit_solution(6447499362397629351)
XLA Ops:
  13.4 48.3 %all-gather.6.cloned.1.call-done = bf16[128,32,256]{2,0,1:T(8,128)(2,1)} async-done(((bf16[8,32,256]{2,0,1:T(8,128)(2,1)}), bf16[128,32,256]{2,0,1:T(8,128)(2,1)}) %all-gather.6.cloned.1.call-update) | async-done | bytes 2097168 | tf_op jit(solution)/shard_map/all_gather | solution.py:99
  68.0 41.2 %all-gather.12.cloned.1.call-done = bf16[128,32,256]{2,0,1:T(8,128)(2,1)} async-done(((bf16[8,32,256]{2,0,1:T(8,128)(2,1)}), bf16[128,32,256]{2,0,1:T(8,128)(2,1)}) %all-gather.12.cloned.1.call-update) | async-done | bytes 2097168 | tf_op jit(solution)/shard_map/all_gather | solution.py:100
  114.2 28.1 %all-gather.10.cloned.1.call-done = bf16[8,256,256]{2,1,0:T(8,128)(2,1)} async-done(((bf16[8,32,256]{2,1,0:T(8,128)(2,1)}), bf16[8,256,256]{2,1,0:T(8,128)(2,1)}) %all-gather.10.cloned.1.call-update) | async-done | bytes 1048592 | tf_op jit(solution)/shard_map/all_gather | solution.py:116
  142.4 40.1 %all-gather.8.cloned.1.call-done = bf16[8,256,256]{2,0,1:T(8,128)(2,1)} async-done(((bf16[8,32,256]{2,0,1:T(8,128)(2,1)}), bf16[8,256,256]{2,0,1:T(8,128)(2,1)}) %all-gather.8.cloned.1.call-update) | async-done | bytes 1048592 | tf_op jit(solution)/shard_map/all_gather | solution.py:115
  182.4 60.4 %while.51 = (s32[]{:T(128)}, f32[32,256]{1,0:T(8,128)S(1)}, f32[32,256]{1,0:T(8,128)S(1)}, f32[8,32,256]{2,1,0:T(8,128)S(1)}, s32[8]{0:T(128)S(1)}, /*index=5*/p...) while((s32[]{:T(128)}, f32[32,256]{1,0:T(8,128)S(1)}, ...), condition=%wide.region_4.5_spmd.clone, body=%wide.region_0.4_spmd.clone.sunk | while | flops 12042247 | bytes 8773351 | solution.py:44
  244.0 122.4 %while.50 = (s32[]{:T(128)}, bf16[8,8,32,32]{2,1,3,0:T(8,128)(2,1)}, bf16[8,8,32,32]{3,2,1,0:T(8,128)(2,1)}, f32[8,8,32,256]{3,1,2,0:T(8,128)}, f32[8,8,32,256]{...) while((s32[]{:T(128)}, ...), condition=%wide.region_10.11_spmd, body=%wide.region_6.10_spmd.sunk | while | flops 73474048 | bytes 12247835 | solution.py:63
  248.9 3.9 fusion.69
  264.2 3.9 fusion.69
  268.7 3.4 fusion.70
  279.5 3.9 fusion.69
  294.8 3.9 fusion.69
  310.1 3.9 fusion.69
  325.4 3.9 fusion.69
  329.9 3.4 fusion.70
  340.7 3.9 fusion.69
  356.0 3.9 fusion.69
  360.5 3.4 fusion.70
  371.0 39.7 %reduce-scatter.5.cloned.1.call-done = f32[8,32,256]{2,0,1:T(8,128)} async-done(((f32[8,256,256]{2,0,1:T(8,128)}), f32[8,32,256]{2,0,1:T(8,128)}) %reduce-scatter.5.cloned.1.call-update) | async-done | bytes 262160 | tf_op jit(solution)/shard_map/reduce_scatter | solution.py:141
  411.7 42.7 %reduce-scatter.3.cloned.1.call-done = f32[8,32,256]{2,0,1:T(8,128)} async-done(((f32[8,256,256]{2,0,1:T(8,128)}), f32[8,32,256]{2,0,1:T(8,128)}) %reduce-scatter.3.cloned.1.call-update) | async-done | bytes 262160 | tf_op jit(solution)/shard_map/reduce_scatter | solution.py:138
  456.3 30.2 %all_gather.18 = bf16[128,512]{0,1:T(8,128)(2,1)S(1)} all-gather(bf16[128,32]{0,1:T(8,128)(2,1)S(1)} %constant_dynamic-update-slice_fusion), channel_id=1, replica_groups=mesh['row'=8,'head'=16] {'head'}, dimensions={1}, use_global_device_ids=true | all-gather | bytes 139264 | tf_op jit(solution)/shard_map/all_gather | solution.py:152
  487.9 25.7 %all-reduce = (f32[128,32]{0,1:T(8,128)S(1)}, f32[8,128]{1,0:T(8,128)}) all-reduce(f32[128,32]{0,1:T(8,128)S(1)} %fusion.30, f32[8,128]{1,0:T(8,128)S(1)} %fusion.31), channel_id=1, replica_groups=mesh['row'=8,'head'=16] {'row'}, use_global_device_ids=true, to_apply=%region_13.14 | all-reduce | flops 5120 | bytes 40960 | tf_op jit(solution)/shard_map/psum | solution.py:166
  514.2 20.6 %all-gather.14.cloned.1.call-done = bf16[512,32,256]{2,0,1:T(8,128)(2,1)} async-done(((bf16[32,32,256]{2,0,1:T(8,128)(2,1)}), bf16[512,32,256]{2,0,1:T(8,128)(2,1)}) %all-gather.14.cloned.1.call-update) | async-done | bytes 8388624 | tf_op jit(solution)/shard_map/all_gather | solution.py:154
  534.8 11.9 %copy.98 = bf16[512,32,256]{0,2,1:T(8,128)(2,1)} copy(bf16[512,32,256]{2,0,1:T(8,128)(2,1)} %all-gather.14.cloned.1.call-done) | data formatting | bytes 16777216 | tf_op jit(solution)/shard_map/all_gather | solution.py:154
  546.7 5.7 %convolution_convert_fusion.1 = bf16[8,8192]{1,0:T(8,128)(2,1)S(1)} fusion(bf16[512,8192]{0,1:T(8,128)(2,1)} %bitcast.93, bf16[128,512]{0,1:T(8,128)(2,1)S(1)} %all_gather.18, s32[]{:T(128)S(6)} %select_n.27), kind=kOutput, calls=%fused_computation.50 | convolution fusion | flops 67174400 | bytes 8650756 | tf_op jit(solution)/shard_map/dot_general | solution.py:156
  (241 shorter events, 158.7 us)
Async XLA Ops:
  7.2 105.3 %copy-start = (bf16[8,128]{1,0:T(8,128)(2,1)S(1)}, bf16[8,128]{1,0:T(8,128)(2,1)}, u32[]{:S(2)}) copy-start(bf16[8,128]{1,0:T(8,128)(2,1)} %param.19) | copy-start | bytes 6148
  7.2 54.5 %all-gather.6.cloned.1.call-start = ((), (), s32[]{:S(2)}) async-start(), calls=%async_computation.2 | async-start | bytes 2228224 | tf_op jit(solution)/shard_map/all_gather | solution.py:99
  8.9 100.3 %all-gather.12.cloned.1.call-start = ((), (), s32[]{:S(2)}) async-start(), calls=%async_computation.5 | async-start | bytes 2228224 | tf_op jit(solution)/shard_map/all_gather | solution.py:100
  10.6 131.8 %all-gather.10.cloned.1.call-start = ((), (), s32[]{:S(2)}) async-start(), calls=%async_computation.4 | async-start | bytes 1179648 | tf_op jit(solution)/shard_map/all_gather | solution.py:116
  64.9 2.9 copy-start.6
  67.1 115.3 %all-gather.8.cloned.1.call-start = ((), (), s32[]{:S(2)}) async-start(), calls=%async_computation.3 | async-start | bytes 1179648 | tf_op jit(solution)/shard_map/all_gather | solution.py:115
  67.7 343.0 %reduce-scatter.5.cloned.1.call-start = ((), (), s32[]{:S(2)}) async-start(), calls=%async_computation.7 | async-start | bytes 2359296 | tf_op jit(solution)/shard_map/reduce_scatter | solution.py:141
  182.4 61.5 %copy-start.3 = (f32[8,8,32,256]{3,2,1,0:T(8,128)S(1)}, f32[8,8,32,256]{3,2,1,0:T(8,128)}, u32[]{:S(2)}) copy-start(f32[8,8,32,256]{3,2,1,0:T(8,128)} %custom-call.7) | copy-start | bytes 6291460
  368.8 1.0 copy-start.4
  368.8 1.4 copy-start.5
  368.9 85.5 %reduce-scatter.3.cloned.1.call-start = ((), (), s32[]{:S(2)}) async-start(), calls=%async_computation.6 | async-start | bytes 2359296 | tf_op jit(solution)/shard_map/reduce_scatter | solution.py:138
  369.4 165.4 %all-gather.14.cloned.1.call-start = ((), (), s32[]{:S(2)}) async-start(), calls=%async_computation.8 | async-start | bytes 8912896 | tf_op jit(solution)/shard_map/all_gather | solution.py:154
  370.3 116.2 %copy-start.1 = (bf16[128,32,256]{2,0,1:T(8,128)(2,1)S(1)}, bf16[128,32,256]{2,0,1:T(8,128)(2,1)}, u32[]{:S(2)}) copy-start(bf16[128,32,256]{2,0,1:T(8,128)(2,1)} %all-gather.12.cloned.1.call-done) | copy-start | bytes 6291460
  456.2 30.9 %copy-start.2 = (bf16[128,32,256]{2,0,1:T(8,128)(2,1)S(1)}, bf16[128,32,256]{2,0,1:T(8,128)(2,1)}, u32[]{:S(2)}) copy-start(bf16[128,32,256]{2,0,1:T(8,128)(2,1)} %all-gather.6.cloned.1.call-done) | copy-start | bytes 6291460
Sparse Core Ops, SparseCore 0:
  10.9 50.7 all-gather.5
  64.0 45.2 all-gather.11
  110.9 31.4 all-gather.9
  144.4 37.9 all-gather.7
  369.0 41.6 reduce-scatter.4
  413.0 41.3 reduce-scatter.2
  456.9 77.8 all-gather.13
where the time goes:
time: 562 us; the launch traced here: 560 us
  waiting for transfers between devices  262 us (47%)
  matrix products  86.6 us (15%)
  other arithmetic  73.1 us (13%)
  local copies, waits for them, and re-layouts  56 us (10%)
  blocking collectives  55.9 us (10%)
  between operations  14.4 us (3%)
  loops' own time  11.7 us (2%)
    all_gather x1, waiting for transfers between devices, local(): lax.all_gather(link_tensor_source, 'head', axis=0, tiled=True)  48.3 us
    reduce_scatter x1, waiting for transfers between devices, local(): lax.psum_scatter(key_terms.reshape(chans, width, width), 'row', scatter_d...  42.7 us
    all_gather x1, waiting for transfers between devices, local(): lax.all_gather(upstream_sensitivity, 'head', axis=0, tiled=True)  41.2 us
    all_gather x1, waiting for transfers between devices, local(): lax.all_gather(key_part, 'row', axis=1, tiled=True)  40.1 us
    reduce_scatter x1, waiting for transfers between devices, local(): lax.psum_scatter(right_terms.reshape(chans, width, width), 'row', scatter...  39.7 us
    dot_general x16, matrix products, scores(): raw = jnp.einsum('cil,clj->ilj', query_block, key_block, precision=HIGH)  31.7 us
    reduce_sum x8, other arithmetic, backward(): (prob[None] * grad_wide[:, :, None, :] * left_block[:, :, :, None]).sum(a...  30.8 us
    all_gather x1, blocking collectives, local(): all_columns = lax.all_gather(w_cat, 'head', axis=1, tiled=True)  30.2 us
  transfers between devices with their start and end apart: 7, of which 7 were waited for; matrix products, arithmetic and copies ran while one was open for 3% of the time, Pallas kernels for 0%

commit v1 on v0

v1 whole, which is shorter than its diff:
```python
import functools

import jax
import jax.numpy as jnp
from jax import lax
from jax.experimental import pallas as pl
from jax.experimental.pallas import tpu as pltpu
from jax.sharding import PartitionSpec as P

F32, BF16 = jnp.float32, jnp.bfloat16
MESH = pl.DeviceIdType.MESH
NT = (((1,), (1,)), ((), ()))
NN = (((1,), (0,)), ((), ()))
TN = (((0,), (0,)), ((), ()))
CH, I, L, J = 8, 64, 256, 128
NX = 8
HEADS, ROWS = 16, 8


def dot(a, b, dims=NN):
    return lax.dot_general(a, b, dims, preferred_element_type=F32)


def core_scratch():
    return dict(
        pt=pltpu.VMEM((1024, 1024), BF16),
        q2=pltpu.VMEM((I, 2048), BF16), b2=pltpu.VMEM((I, 2048), BF16),
        qt=pltpu.VMEM((2048, 128), BF16), kf=pltpu.VMEM((2048, J), F32), rf=pltpu.VMEM((2048, J), F32),
        k2=pltpu.VMEM((2048, J), BF16), mt=pltpu.VMEM((16, 256), BF16), wc=pltpu.VMEM((128, 1024), BF16), lb16=pltpu.VMEM((I, 2048), BF16), rg=pltpu.VMEM((2048, J), BF16),
        s=pltpu.VMEM((L, I, J), F32), m=pltpu.VMEM((I, J), F32), gs=pltpu.VMEM((CH, I, J), F32), ds=pltpu.VMEM((I, J), F32),
        mix=pltpu.VMEM((CH, I, J), F32), tot=pltpu.VMEM((I, J), F32),
        e=pltpu.VMEM((16, I, J), F32), br8=pltpu.VMEM((2, 64, J), F32), br2=pltpu.VMEM((2048, J), F32), bk2=pltpu.VMEM((2048, J), F32),
    )


def permutation(pt):
    @pl.loop(0, 8)
    def _(n):
        a = lax.broadcasted_iota(jnp.int32, (128, 1024), 0) + n * 128
        b = lax.broadcasted_iota(jnp.int32, (128, 1024), 1)
        hit = ((a >> 3) == (b & 127)) & ((a & 7) == (b >> 7))
        pt[pl.ds(pl.multiple_of(n * 128, 128), 128), :] = jnp.where(hit, 1.0, 0.0).astype(BF16)

def core(ql, kr, gg, fac, bq2, bl2, mixed, w, after=None):
    permutation(w["pt"])
    pt = w["pt"]
    row = lax.broadcasted_iota(jnp.int32, (16, 256), 0)
    lane = lax.broadcasted_iota(jnp.int32, (16, 256), 1)
    w["mt"][...] = jnp.where(((lane & 127) >> 3) == row, 1.0, 0.0).astype(BF16)
    ra = lax.broadcasted_iota(jnp.int32, (128, 1024), 0)
    rb_ = lax.broadcasted_iota(jnp.int32, (128, 1024), 1)
    w["wc"][...] = jnp.where((ra & 7) == (rb_ >> 7), 1.0, 0.0).astype(BF16)
    for half in range(2):
        cut = slice(half * 128, half * 128 + 128)
        out = slice(half * 1024, half * 1024 + 1024)
        both = lambda c: jnp.concatenate([ql[0, c, :, cut], ql[1, c, :, cut]], axis=0)
        qcat = jnp.concatenate([both(c) for c in range(CH)], axis=1)
        lcat = jnp.concatenate([both(CH + c) for c in range(CH)], axis=1)
        bcat = jnp.concatenate([both(2 * CH), jnp.zeros((I, 896), BF16)], axis=1)
        got = dot(jnp.concatenate([qcat, lcat, bcat], axis=0), pt[...], NT)
        w["q2"][:, out] = got[:I].astype(BF16)
        w["lb16"][:, out] = got[I:2 * I].astype(BF16)
        w["b2"][:, out] = got[2 * I:].astype(BF16)
        w["qt"][out, :] = dot(pt[...], jnp.concatenate([qcat, qcat], axis=0), NT).astype(BF16)
    for c in range(CH):
        for z in range(8):
            w["kf"][pl.ds(z * 256 + c, 32, stride=8), :] = kr[z, c].astype(F32)
            w["rf"][pl.ds(z * 256 + c, 32, stride=8), :] = kr[z, CH + c].astype(F32)
    w["k2"][...] = w["kf"][...].astype(BF16)
    w["rg"][...] = w["rf"][...].astype(BF16)
    w["m"][...] = jnp.full((I, J), -3e38, F32)

    @pl.loop(0, 16)
    def _(n):
        at = pl.ds(pl.multiple_of(n * 128, 128), 128)
        qb = jnp.concatenate([w["q2"][:, at], w["b2"][:, at]], axis=1)
        kk = jnp.concatenate([w["k2"][at, :], jnp.ones((128, J), BF16)], axis=0)
        lhs = jnp.concatenate([qb * w["mt"][t:t + 1, :] for t in range(16)], axis=0)
        raw = dot(lhs, kk).reshape(16, I, J)
        top = w["m"][...]
        for t in range(16):
            top = jnp.maximum(top, raw[t])
        w["m"][...] = top
        w["s"][pl.ds(n * 16, 16)] = raw

    f = fac[0]

    @pl.loop(0, 4)
    def _(ip):
        rows = pl.ds(pl.multiple_of(ip * 16, 16), 16)
        top = w["m"][rows, :]

        def step(n, carry):
            total, acc = carry
            acc = list(acc)
            tile = w["lb16"][rows, pl.ds(pl.multiple_of(n * 128, 128), 128)]
            lhs = jnp.concatenate([tile * w["mt"][t:t + 1, :128] for t in range(16)], axis=0)
            spread = dot(lhs, w["wc"][...])
            for t in range(16):
                lv = n * 16 + t
                wt = jnp.exp(f * (w["s"][lv, rows, :] - top))
                w["s"][lv, rows, :] = wt
                total = total + wt
                rr = w["rf"][pl.ds(pl.multiple_of(lv * 8, 8), 8), :]
                for c in range(CH):
                    lb = spread[t * 16:t * 16 + 16, c * 128:c * 128 + 128]
                    acc[c] = acc[c] + (wt * rr[c:c + 1, :]) * lb
            return total, tuple(acc)

        zero = jnp.zeros((16, J), F32)
        total, acc = lax.fori_loop(0, 16, step, (zero, (zero,) * CH))
        inv = 1.0 / total
        delta = zero
        for c in range(CH):
            gc = gg[ip >> 1, c, pl.ds(pl.multiple_of((ip & 1) * 16, 16), 16), :].astype(F32)
            mc = acc[c] * inv
            mixed[c, rows, :] = mc.astype(BF16)
            delta = delta + gc * mc
            w["gs"][c, rows, :] = gc * inv
        w["ds"][rows, :] = delta * inv

    lanes = lax.broadcasted_iota(jnp.int32, (8, 128), 1)

    @pl.loop(0, 16)
    def _(n):
        at = pl.ds(pl.multiple_of(n * 128, 128), 128)
        bl2[:, at] = jnp.zeros((I, 128), F32)

        rg = w["rg"][at, :]
        rdup = jnp.concatenate([rg, rg], axis=1)

        @pl.loop(0, 16, unroll=4)
        def _(t):
            lv = n * 16 + t
            lanes64 = lax.broadcasted_iota(jnp.int32, (I, 128), 1)
            pick = jnp.where((lanes64 >> 3) == t, 1.0, 0.0).astype(BF16)
            spread = dot(w["lb16"][:, at] * pick, w["wc"][...])
            rr = w["rf"][pl.ds(pl.multiple_of(lv * 8, 8), 8), :]
            rb = [jnp.broadcast_to(rr[c:c + 1, :], (8, J)) for c in range(CH)]
            br = [jnp.zeros((8, J), F32) for c in range(CH)]
            base = t * 8
            halves = [[] for c in range(CH)]
            for it in range(8):
                rows = slice(it * 8, it * 8 + 8)
                wt = w["s"][lv, rows, :]
                pgp = None
                for c in range(CH):
                    x = wt * w["gs"][c, rows, :]
                    xl = x * spread[rows, c * 128:c * 128 + 128]
                    br[c] = br[c] + xl
                    term = xl * rb[c]
                    pgp = term if pgp is None else pgp + term
                    halves[c].append(x)
                w["e"][t, rows, :] = pgp - wt * w["ds"][rows, :]
            blt = bl2[:, at]
            for c in range(CH):
                if c < NX:
                    red = jnp.sum(jnp.concatenate(halves[c], axis=0) * rr[c:c + 1, :], axis=1, keepdims=True)
                else:
                    xc = jnp.concatenate(halves[c], axis=0)
                    xh = xc.astype(BF16)
                    xo = (xc - xh.astype(F32)).astype(BF16)
                    red = dot(jnp.concatenate([xh, xo], axis=1), rdup, NT)
                blt = jnp.where(lanes64 == base + c, red, blt)
            bl2[:, at] = blt
            slot = lax.rem(t, 2)
            for c in range(CH):
                w["br8"][slot, c * 8:c * 8 + 8, :] = br[c]
            tot = w["br8"][slot, pl.ds(0, 8, stride=8), :]
            for z in range(1, 8):
                tot = tot + w["br8"][slot, pl.ds(z, 8, stride=8), :]
            w["br2"][pl.ds(pl.multiple_of(lv * 8, 8), 8), :] = tot

        ev = w["e"][...].reshape(16 * I, J)
        hi = ev.astype(BF16)
        lo = (ev - hi.astype(F32)).astype(BF16)
        kt = w["k2"][at, :]
        bqw = dot(jnp.concatenate([hi, lo], axis=1), jnp.concatenate([kt, kt], axis=1), NT)
        tot = jnp.zeros((I, 128), F32)
        lane2 = lax.broadcasted_iota(jnp.int32, (I, 128), 1)
        for t in range(16):
            tot = jnp.where((lane2 >> 3) == t, bqw[t * I:(t + 1) * I, :], tot)
        bq2[:, at] = f * tot
        sub_r = lax.broadcasted_iota(jnp.int32, (32, 256), 0)
        sub_c = lax.broadcasted_iota(jnp.int32, (32, 256), 1)
        keep = jnp.where((sub_r >> 3) == (sub_c >> 6), 1.0, 0.0).astype(BF16)
        for u in range(4):
            qrow = w["qt"][pl.ds(pl.multiple_of(n * 128 + u * 32, 32), 32), :]
            lhs = jnp.concatenate([qrow, qrow], axis=1) * keep
            part = dot(jnp.concatenate([lhs, lhs], axis=1), jnp.concatenate([hi[u * 256:u * 256 + 256], lo[u * 256:u * 256 + 256]], axis=0))
            w["bk2"][pl.ds(pl.multiple_of(n * 128 + u * 32, 32), 32), :] = f * part
        if after is not None:
            after(n)


def greet(groups):
    barrier = pltpu.get_barrier_semaphore()
    count = 0
    for axis, n in groups:
        me = lax.axis_index(axis)

        @pl.loop(1, n)
        def _(s):
            pl.semaphore_signal(barrier, inc=1, device_id={axis: lax.rem(me + s, n)}, device_id_type=MESH)

        count += n - 1
    pl.semaphore_wait(barrier, count)


class Trade:
    def __init__(self, axis, n, src, dst, send_sem, recv_sem):
        self.axis, self.n, self.src, self.dst, self.send_sem, self.recv_sem = axis, n, src, dst, send_sem, recv_sem
        self.me = lax.axis_index(axis)

    def copy(self, s):
        peer = lax.rem(self.me + s, self.n)
        return pltpu.make_async_remote_copy(
            src_ref=self.src(peer), dst_ref=self.dst(self.me), send_sem=self.send_sem.at[s], recv_sem=self.recv_sem.at[s],
            device_id={self.axis: peer}, device_id_type=MESH)

    def start(self):
        @pl.loop(1, self.n)
        def _(s):
            self.copy(s).start()

    def finish(self):
        @pl.loop(1, self.n)
        def _(s):
            self.copy(s).wait_recv()

    def drain(self):
        @pl.loop(1, self.n)
        def _(s):
            self.copy(s).wait_send()


def to_pairs(wide, stage, count):
    for i in range(32):
        for z in range(2):
            at = (i % 2) * 256 + z * 128
            stage[i // 2, :, at:at + 128] = wide[z, pl.ds(i, count, stride=32), :].astype(BF16)


def from_pairs(recv, wide, count):
    for i in range(32):
        for z in range(2):
            at = (i % 2) * 256 + z * 128
            wide[z, pl.ds(i, count, stride=32), :] = recv[i // 2, :, at:at + 128][:count].astype(F32)


def project_kernel(x, u, wself, nat, gathered, wall, xs, stage1, stage2, recv2, natf, sems):
    me = lax.axis_index("head")
    for z in range(2):
        xs[z, 0:256, :] = x[:, :, z * 128:z * 128 + 128].reshape(256, 128).astype(F32)
        xs[z, 256:512, :] = u[:, :, z * 128:z * 128 + 128].reshape(256, 128).astype(F32)
    to_pairs(xs, stage1, 16)
    greet([("head", HEADS)])
    first = Trade("head", HEADS, lambda p: stage1.at[p], lambda p: gathered.at[p], sems.at[0], sems.at[1])
    weights = Trade("head", HEADS, lambda p: wself, lambda p: wall.at[p], sems.at[2], sems.at[3])
    first.start()
    weights.start()
    gathered[me] = stage1[me]
    wall[me] = wself[...]
    first.finish()
    weights.finish()
    mapped = dot(wall[...].reshape(768, 256), gathered[...].reshape(256, 512))
    stage2[...] = mapped.astype(BF16).reshape(16, 48, 512)
    second = Trade("head", HEADS, lambda p: stage2.at[p], lambda p: recv2.at[p], sems.at[4], sems.at[5])
    second.start()
    recv2[me] = stage2[me]
    second.finish()
    from_pairs(recv2, natf, 40)
    for z in range(2):
        nat[:, :, z * 128:z * 128 + 128] = natf[z].astype(BF16).reshape(40, 32, 128)
    first.drain()
    weights.drain()
    second.drain()


def attention_kernel(names, nat, bias, fac, backs, ql, kr, gg, ql2, qlin, kro, krin, mx, mixin, sems, psems, *scratch):
    w = dict(zip(names, scratch))
    me = lax.axis_index("row")
    jb = lax.rem(me, 2)
    partner = me + 1 - 2 * jb
    pj = 1 - jb

    def half(j):
        return pl.ds(pl.multiple_of(j * 128, 128), 128)

    def to_partner(n, src, dst):
        return pltpu.make_async_remote_copy(src_ref=src, dst_ref=dst, send_sem=psems.at[0, n], recv_sem=psems.at[1, n],
                                            device_id={"row": partner}, device_id_type=MESH)

    greet([("row", ROWS)])
    pairs_in = Trade("row", ROWS, lambda p: kr_src.at[:, :, half(lax.rem(p, 2))], lambda p: kr.at[p], sems.at[0], sems.at[1])
    kr_src = nat.at[pl.ds(0, 16)]
    ahead = [
        to_partner(0, nat.at[pl.ds(16, 16)], ql.at[jb, pl.ds(0, 16)]),
        to_partner(1, bias, ql.at[jb, 16]),
        to_partner(2, nat.at[pl.ds(32, 8), :, half(pj)], gg.at[jb]),
    ]
    for copy in ahead:
        copy.start()
    pairs_in.start()
    ql[jb, 0:16] = nat[16:32]
    ql[jb, 16] = bias[...]
    gg[jb] = nat[32:40, :, half(jb)]
    kr[me] = nat[0:16, :, half(jb)]
    for copy in ahead:
        copy.wait()
    pairs_in.finish()
    core(ql, kr, gg, fac, ql2.at[0], ql2.at[1], mx, w)
    for z in range(8):
        for c in range(CH):
            kro[z, c] = w["bk2"][pl.ds(z * 256 + c, 32, stride=8), :]
            kro[z, CH + c] = w["br2"][pl.ds(z * 256 + c, 32, stride=8), :]
    pairs_out = Trade("row", ROWS, lambda p: kro.at[p], lambda p: krin.at[p], sems.at[2], sems.at[3])
    other = pl.ds(pl.multiple_of(pj * 32, 32), 32)
    own = pl.ds(pl.multiple_of(jb * 32, 32), 32)
    back = [to_partner(3, ql2.at[:, other], qlin), to_partner(4, mx.at[:, other], mixin)]
    for copy in back:
        copy.start()
    pairs_out.start()
    krin[me] = kro[me]
    for copy in back:
        copy.wait()
    both = (ql2[:, own, :] + qlin[...]).astype(BF16).reshape(64, 2048)
    for h in range(2):
        plain = dot(both[:, h * 1024:h * 1024 + 1024], w["pt"][...]).astype(BF16)
        for c in range(CH):
            backs[16 + c, :, h * 128:h * 128 + 128] = plain[0:32, c * 128:c * 128 + 128]
            backs[24 + c, :, h * 128:h * 128 + 128] = plain[32:64, c * 128:c * 128 + 128]
    backs[32:40, :, half(jb)] = mx[:, own, :]
    backs[32:40, :, half(pj)] = mixin[...]
    pairs_out.finish()
    for j in range(2):
        total = krin[j] + krin[2 + j] + krin[4 + j] + krin[6 + j]
        total = total.astype(BF16)
        backs[0:16, :, j * 128:j * 128 + 128] = total
    pairs_in.drain()
    pairs_out.drain()


def gradient_kernel(backs, gathered, wall, grads, weights, bf, stage3, recv3, stage4, recv4, gw, gwin, part, gwrow, gf, sems):
    me, row = lax.axis_index("head"), lax.axis_index("row")
    for z in range(2):
        bf[z, 0:1280, :] = backs[:, :, z * 128:z * 128 + 128].reshape(1280, 128).astype(F32)
        bf[z, 1280:1536, :] = jnp.zeros((256, 128), F32)
    to_pairs(bf, stage3, 48)
    greet([("head", HEADS), ("row", ROWS)])
    first = Trade("head", HEADS, lambda p: stage3.at[p], lambda p: recv3.at[p], sems.at[0], sems.at[1])
    first.start()
    recv3[me] = stage3[me]
    first.finish()
    every = recv3[...].reshape(768, 512)
    gw[...] = dot(every, gathered[...].reshape(256, 512), NT).reshape(16, 48, 256)
    sums = Trade("head", HEADS, lambda p: gw.at[p, pl.ds(0, 40)], lambda p: gwin.at[p], sems.at[2], sems.at[3])
    sums.start()
    gwin[me] = gw[me, 0:40, :]
    stage4[...] = dot(wall[...].reshape(768, 256), every, TN).astype(BF16).reshape(16, 16, 512)
    second = Trade("head", HEADS, lambda p: stage4.at[p], lambda p: recv4.at[p], sems.at[4], sems.at[5])
    second.start()
    recv4[me] = stage4[me]
    sums.finish()
    total = gwin[0]
    for p in range(1, 16):
        total = total + gwin[p]
    part[...] = total
    last = Trade("row", ROWS, lambda p: part, lambda p: gwrow.at[p], sems.at[6], sems.at[7])
    last.start()
    gwrow[row] = total
    second.finish()
    from_pairs(recv4, gf, 8)
    for z in range(2):
        grads[:, :, z * 128:z * 128 + 128] = gf[z].astype(BF16).reshape(8, 32, 128)
    last.finish()
    total = gwrow[0]
    for p in range(1, 8):
        total = total + gwrow[p]
    weights[...] = total * (1.0 / 256.0)
    for trade in (first, sums, second, last):
        trade.drain()


VM = pl.BlockSpec(memory_space=pltpu.VMEM)


def params(number):
    return pltpu.CompilerParams(collective_id=number, has_side_effects=True, vmem_limit_bytes=56 * 2 ** 20)


def local(x, allowance, asking, lookup, first_content, second_content, final, scaling, upstream):
    order = [lookup, second_content, asking, first_content]
    rows = jnp.concatenate(order, axis=1).T.reshape(32, 16, 1, 8)
    from_x = jnp.concatenate([rows, jnp.zeros_like(rows)], axis=2).reshape(32, 256)
    rows = final.reshape(8, 16, 1, 8)
    from_u = jnp.concatenate([jnp.zeros_like(rows), rows], axis=2).reshape(8, 256)
    wself = jnp.concatenate([from_x, from_u, jnp.zeros((8, 256), BF16)], axis=0)
    node = lax.axis_index("row") * 32 + lax.broadcasted_iota(jnp.int32, (32, 256), 0)
    valid = (allowance == 1) | (node == lax.broadcasted_iota(jnp.int32, (32, 256), 1))
    bias = jnp.where(valid, 0.0, -1e30).astype(BF16)

    dma = pltpu.SemaphoreType.DMA
    nat, gathered, wall = pl.pallas_call(
        project_kernel,
        out_shape=[jax.ShapeDtypeStruct((40, 32, 256), BF16), jax.ShapeDtypeStruct((16, 16, 512), BF16),
                   jax.ShapeDtypeStruct((16, 48, 256), BF16)],
        in_specs=[VM] * 3, out_specs=[VM] * 3,
        scratch_shapes=[pltpu.VMEM((2, 512, 128), F32), pltpu.VMEM((16, 16, 512), BF16), pltpu.VMEM((16, 48, 512), BF16),
                        pltpu.VMEM((16, 48, 512), BF16), pltpu.VMEM((2, 1280, 128), F32), dma((6, 16))],
        compiler_params=params(0), name="project",
    )(x, upstream, wself)

    names = core_scratch()
    backs = pl.pallas_call(
        functools.partial(attention_kernel, list(names)),
        out_shape=jax.ShapeDtypeStruct((40, 32, 256), BF16),
        in_specs=[VM, VM, pl.BlockSpec(memory_space=pltpu.SMEM)], out_specs=VM,
        scratch_shapes=[
            pltpu.VMEM((2, 17, 32, 256), BF16), pltpu.VMEM((8, 16, 32, 128), BF16), pltpu.VMEM((2, 8, 32, 128), BF16),
            pltpu.VMEM((2, 64, 2048), F32), pltpu.VMEM((2, 32, 2048), F32),
            pltpu.VMEM((8, 16, 32, 128), F32), pltpu.VMEM((8, 16, 32, 128), F32),
            pltpu.VMEM((8, 64, 128), BF16), pltpu.VMEM((8, 32, 128), BF16), dma((4, 8)), dma((2, 5)),
        ] + list(names.values()),
        compiler_params=params(1), name="attention",
    )(nat, bias, scaling)

    grads, weights = pl.pallas_call(
        gradient_kernel,
        out_shape=[jax.ShapeDtypeStruct((8, 32, 256), BF16), jax.ShapeDtypeStruct((40, 256), F32)],
        in_specs=[VM] * 3, out_specs=[VM] * 2,
        scratch_shapes=[
            pltpu.VMEM((2, 1536, 128), F32), pltpu.VMEM((16, 48, 512), BF16), pltpu.VMEM((16, 48, 512), BF16),
            pltpu.VMEM((16, 16, 512), BF16), pltpu.VMEM((16, 16, 512), BF16),
            pltpu.VMEM((16, 48, 256), F32), pltpu.VMEM((16, 40, 256), F32), pltpu.VMEM((40, 256), F32),
            pltpu.VMEM((8, 40, 256), F32), pltpu.VMEM((2, 256, 128), F32), dma((8, 16)),
        ],
        compiler_params=params(2), name="gradient",
    )(backs, gathered, wall)
    split = weights.reshape(5, 8, 16, 2, 8)
    of_x = split[:4, :, :, 0, :].reshape(4, 8, 128)
    of_u = split[4, :, :, 1, :].reshape(8, 128)
    return grads, of_x[2].T, of_x[0].T, of_x[3].T, of_x[1].T, of_u


def solution(mesh):
    pairs, columns = P("head", "row", None), P(None, "head")
    placed = (pairs, P("row", None), columns, columns, columns, columns, P("head", None), P("head"), pairs)
    return jax.shard_map(
        local, mesh=mesh, in_specs=placed,
        out_specs=(pairs, columns, columns, columns, columns, P("head", None)), check_vma=False,
    )
```

time: 562 us -> 215 us (0.38)
  waiting for transfers between devices: 262 us -> 0 us
  Pallas kernels: 0 us -> 203 us
  matrix products: 86.6 us -> 0 us
  other arithmetic: 73.1 us -> 2.09 us
  blocking collectives: 55.9 us -> 0 us
  local copies, waits for them, and re-layouts: 56 us -> 8 us
  between operations: 14.4 us -> 1.39 us
  loops' own time: 11.7 us -> 0 us
    pallas_call x0 -> x3, Pallas kernels: none -> 203 us  [the longest x1 130 us: local(): pl.pallas_call(functools.partial(attention_kernel, list(names)), out_shap...]
    all_gather x5 -> x0, waiting for transfers between devices: 178 us -> none  [the longest x1 48.3 us: local(): lax.all_gather(link_tensor_source, 'head', axis=0, tiled=True)]
    dot_general x37 -> x0, matrix products: 86.6 us -> none  [the longest x16 31.7 us: scores(): raw = jnp.einsum('cil,clj->ilj', query_block, key_block, precision=HIGH)]
    reduce_scatter x2 -> x0, waiting for transfers between devices: 82.4 us -> none  [the longest x1 42.7 us: local(): lax.psum_scatter(key_terms.reshape(chans, width, width), 'row', scatter_d...]
    reduce_sum x24 -> x0, other arithmetic: 50.9 us -> none  [the longest x8 30.8 us: backward(): (prob[None] * grad_wide[:, :, None, :] * left_block[:, :, :, None]).sum(a...]
    all_gather x1 -> x0, blocking collectives: 30.2 us -> none  [local(): all_columns = lax.all_gather(w_cat, 'head', axis=1, tiled=True)]
    psum x1 -> x0, blocking collectives: 25.7 us -> none  [local(): lax.psum((partial_weights * inverse, partial_out * inverse), 'row')]
    convert_element_type x36 -> x1, other arithmetic: 20.2 us -> 0.67 us  [local(): bias = jnp.where(valid, 0.0, -1e+30).astype(BF16)]
  transfers between devices with their start and end apart: 7 -> 0, of which waited for: 7 -> 0; matrix products, arithmetic and copies ran while one was open for 3% -> 0% of each run, Pallas kernels for 0% -> 0%
where the time goes in v1:
time: 215 us
  Pallas kernels  203 us (94%)
  local copies, waits for them, and re-layouts  8 us (4%)
    pallas_call x1, Pallas kernels, local(): pl.pallas_call(functools.partial(attention_kernel, list(names)), out_shap...  130 us
    pallas_call x1, Pallas kernels, local(): pl.pallas_call(gradient_kernel, out_shape=[jax.ShapeDtypeStruct((8, 32, 2...  39.1 us
    pallas_call x1, Pallas kernels, local(): pl.pallas_call(project_kernel, out_shape=[jax.ShapeDtypeStruct((40, 32, 2...  34.2 us

profile of v1, /device:TPU:1, one launch (start us, length us, event | category | flops | bytes accessed | tf_op | source)
XLA Modules:
  0.0 214.6 jit_solution(8413655089671549686)
XLA Ops:
  0.6 0.0 copy-start.1
  1.3 0.1 pad.4.clone
  1.4 0.7 pad_maximum_fusion
  2.1 0.0 copy-done.1
  2.1 0.7 select_convert_fusion.bias
  2.8 0.1 copy.24
  3.0 0.0 copy-start.2
  3.0 0.1 copy.27
  3.0 0.6 copy-done.2
  3.6 0.1 reshape.40
  3.8 0.1 concatenate.14.clone
  3.9 0.1 reshape.38
  4.0 0.7 maximum_maximum_fusion.wself
  4.7 34.2 %project.1 = (bf16[40,32,256]{2,1,0:T(8,128)(2,1)}, bf16[16,16,512]{2,1,0:T(8,128)(2,1)}, bf16[16,48,256]{2,1,0:T(8,128)(2,1)}) custom-call(bf16[8,32,256]{2,1,0:T(8,128)(2,1)} %x.5, bf16[8,32,256]{2,1,0:T(8,128)(2,1)} %u.1, bf16[48,256]{1,0:T(8,128)(2,1)} %maximum_maximum_fusion.wself), custom_call_target="tpu_custom_call" | custom-call | tf_op jit(solution)/shard_map/project/pallas_call | solution.py:404
  38.9 129.8 %attention.1.backs = bf16[40,32,256]{2,1,0:T(8,128)(2,1)} custom-call(bf16[40,32,256]{2,1,0:T(8,128)(2,1)} %get-tuple-element.11.nat, bf16[32,256]{1,0:T(8,128)(2,1)} %select_convert_fusion.bias, f32[1]{0:T(128)S(6)} %copy.31.fac), custom_call_target="tpu_custom_call" | custom-call | tf_op jit(solution)/shard_map/attention/pallas_call | solution.py:415
  168.7 39.1 %gradient.1 = (bf16[8,32,256]{2,1,0:T(8,128)(2,1)}, f32[40,256]{1,0:T(8,128)}) custom-call(bf16[40,32,256]{2,1,0:T(8,128)(2,1)} %attention.1.backs, bf16[16,16,512]{2,1,0:T(8,128)(2,1)} %get-tuple-element.12.gathered, bf16[16,48,256]{2,1,0:T(8,128)(2,1)} %get-tuple-element.13.wall), custom_call_target="tpu_custom_call" | custom-call | tf_op jit(solution)/shard_map/gradient/pallas_call | solution.py:428
  207.8 1.8 reshape.39
  209.6 0.9 slice_reduce_fusion
  210.5 0.7 reshape_squeeze.4
  211.2 0.7 squeeze.15
  211.9 0.7 squeeze.14
  212.6 0.7 squeeze.13
  213.2 0.7 squeeze.12
  213.9 0.7 copy.32
  (5 shorter events, 0.0 us)
Async XLA Ops:
  0.6 1.5 copy-start.1
  3.0 0.7 copy-start.2
  211.2 2.7 %copy-start = (bf16[8,32,256]{2,1,0:T(8,128)(2,1)S(1)}, bf16[8,32,256]{2,1,0:T(8,128)(2,1)}, u32[]{:S(2)}) copy-start(bf16[8,32,256]{2,1,0:T(8,128)(2,1)} %get-tuple-element.27) | copy-start | bytes 393220

commit v2 on v1

v2 whole, which is shorter than its diff:
```python
import functools

import jax
import jax.numpy as jnp
from jax import lax
from jax.experimental import pallas as pl
from jax.experimental.pallas import tpu as pltpu
from jax.sharding import PartitionSpec as P

F32, BF16 = jnp.float32, jnp.bfloat16
MESH = pl.DeviceIdType.MESH
NT = (((1,), (1,)), ((), ()))
NN = (((1,), (0,)), ((), ()))
TN = (((0,), (0,)), ((), ()))
CH, I, L, J = 8, 64, 256, 128
NX = 8
HEADS, ROWS = 16, 8


def dot(a, b, dims=NN):
    return lax.dot_general(a, b, dims, preferred_element_type=F32)


def core_scratch():
    return dict(
        pt=pltpu.VMEM((1024, 1024), BF16),
        q2=pltpu.VMEM((I, 2048), BF16), b2=pltpu.VMEM((I, 2048), BF16),
        qt=pltpu.VMEM((2048, 128), BF16), kf=pltpu.VMEM((2048, J), F32), rf=pltpu.VMEM((2048, J), F32),
        k2=pltpu.VMEM((2048, J), BF16), mt=pltpu.VMEM((16, 256), BF16), wc=pltpu.VMEM((128, 1024), BF16), lb16=pltpu.VMEM((I, 2048), BF16), rg=pltpu.VMEM((2048, J), BF16),
        s=pltpu.VMEM((L, I, J), F32), m=pltpu.VMEM((I, J), F32), gs=pltpu.VMEM((CH, I, J), F32), ds=pltpu.VMEM((I, J), F32),

        e=pltpu.VMEM((16, I, J), F32), br8=pltpu.VMEM((2, 64, J), F32), br2=pltpu.VMEM((256, J), F32), bk2=pltpu.VMEM((256, J), F32),
    )


def permutation(pt):
    @pl.loop(0, 8)
    def _(n):
        a = lax.broadcasted_iota(jnp.int32, (128, 1024), 0) + n * 128
        b = lax.broadcasted_iota(jnp.int32, (128, 1024), 1)
        hit = ((a >> 3) == (b & 127)) & ((a & 7) == (b >> 7))
        pt[pl.ds(pl.multiple_of(n * 128, 128), 128), :] = jnp.where(hit, 1.0, 0.0).astype(BF16)


def constants(w):
    permutation(w["pt"])
    row = lax.broadcasted_iota(jnp.int32, (16, 256), 0)
    lane = lax.broadcasted_iota(jnp.int32, (16, 256), 1)
    w["mt"][...] = jnp.where(((lane & 127) >> 3) == row, 1.0, 0.0).astype(BF16)
    ra = lax.broadcasted_iota(jnp.int32, (128, 1024), 0)
    rb_ = lax.broadcasted_iota(jnp.int32, (128, 1024), 1)
    w["wc"][...] = jnp.where((ra & 7) == (rb_ >> 7), 1.0, 0.0).astype(BF16)


def scores(ql, kr, w):
    pt = w["pt"]
    for half in range(2):
        cut = slice(half * 128, half * 128 + 128)
        out = slice(half * 1024, half * 1024 + 1024)
        both = lambda c: jnp.concatenate([ql[0, c, :, cut], ql[1, c, :, cut]], axis=0)
        qcat = jnp.concatenate([both(c) for c in range(CH)], axis=1)
        lcat = jnp.concatenate([both(CH + c) for c in range(CH)], axis=1)
        bcat = jnp.concatenate([both(2 * CH), jnp.zeros((I, 896), BF16)], axis=1)
        got = dot(jnp.concatenate([qcat, lcat, bcat], axis=0), pt[...], NT)
        w["q2"][:, out] = got[:I].astype(BF16)
        w["lb16"][:, out] = got[I:2 * I].astype(BF16)
        w["b2"][:, out] = got[2 * I:].astype(BF16)
        w["qt"][out, :] = dot(pt[...], jnp.concatenate([qcat, qcat], axis=0), NT).astype(BF16)
    for c in range(CH):
        for z in range(8):
            w["kf"][pl.ds(z * 256 + c, 32, stride=8), :] = kr[z, c].astype(F32)
            w["rf"][pl.ds(z * 256 + c, 32, stride=8), :] = kr[z, CH + c].astype(F32)
    w["k2"][...] = w["kf"][...].astype(BF16)
    w["rg"][...] = w["rf"][...].astype(BF16)
    w["m"][...] = jnp.full((I, J), -3e38, F32)

    @pl.loop(0, 16)
    def _(n):
        at = pl.ds(pl.multiple_of(n * 128, 128), 128)
        qb = jnp.concatenate([w["q2"][:, at], w["b2"][:, at]], axis=1)
        kk = jnp.concatenate([w["k2"][at, :], jnp.ones((128, J), BF16)], axis=0)
        lhs = jnp.concatenate([qb * w["mt"][t:t + 1, :] for t in range(16)], axis=0)
        raw = dot(lhs, kk).reshape(16, I, J)
        top = w["m"][...]
        for t in range(16):
            top = jnp.maximum(top, raw[t])
        w["m"][...] = top
        w["s"][pl.ds(n * 16, 16)] = raw


def forward(gg, f, mixed, w):
    @pl.loop(0, 4)
    def _(ip):
        rows = pl.ds(pl.multiple_of(ip * 16, 16), 16)
        top = w["m"][rows, :]

        def step(n, carry):
            total, acc = carry
            acc = list(acc)
            tile = w["lb16"][rows, pl.ds(pl.multiple_of(n * 128, 128), 128)]
            lhs = jnp.concatenate([tile * w["mt"][t:t + 1, :128] for t in range(16)], axis=0)
            spread = dot(lhs, w["wc"][...])
            for t in range(16):
                lv = n * 16 + t
                wt = jnp.exp(f * (w["s"][lv, rows, :] - top))
                w["s"][lv, rows, :] = wt
                total = total + wt
                rr = w["rf"][pl.ds(pl.multiple_of(lv * 8, 8), 8), :]
                for c in range(CH):
                    lb = spread[t * 16:t * 16 + 16, c * 128:c * 128 + 128]
                    acc[c] = acc[c] + (wt * rr[c:c + 1, :]) * lb
            return total, tuple(acc)

        zero = jnp.zeros((16, J), F32)
        total, acc = lax.fori_loop(0, 16, step, (zero, (zero,) * CH))
        inv = 1.0 / total
        delta = zero
        for c in range(CH):
            gc = gg[ip >> 1, c, pl.ds(pl.multiple_of((ip & 1) * 16, 16), 16), :].astype(F32)
            mc = acc[c] * inv
            mixed[c, rows, :] = mc.astype(BF16)
            delta = delta + gc * mc
            w["gs"][c, rows, :] = gc * inv
        w["ds"][rows, :] = delta * inv


def backward(n, block, f, bq2, bl2, w):
    at = pl.ds(pl.multiple_of(n * 128, 128), 128)
    bl2[:, at] = jnp.zeros((I, 128), F32)

    rg = w["rg"][at, :]
    rdup = jnp.concatenate([rg, rg], axis=1)

    @pl.loop(0, 16, unroll=4)
    def _(t):
        lv = n * 16 + t
        lanes64 = lax.broadcasted_iota(jnp.int32, (I, 128), 1)
        pick = jnp.where((lanes64 >> 3) == t, 1.0, 0.0).astype(BF16)
        spread = dot(w["lb16"][:, at] * pick, w["wc"][...])
        rr = w["rf"][pl.ds(pl.multiple_of(lv * 8, 8), 8), :]
        rb = [jnp.broadcast_to(rr[c:c + 1, :], (8, J)) for c in range(CH)]
        br = [jnp.zeros((8, J), F32) for c in range(CH)]
        base = t * 8
        halves = [[] for c in range(CH)]
        for it in range(8):
            rows = slice(it * 8, it * 8 + 8)
            wt = w["s"][lv, rows, :]
            pgp = None
            for c in range(CH):
                x = wt * w["gs"][c, rows, :]
                xl = x * spread[rows, c * 128:c * 128 + 128]
                br[c] = br[c] + xl
                term = xl * rb[c]
                pgp = term if pgp is None else pgp + term
                halves[c].append(x)
            w["e"][t, rows, :] = pgp - wt * w["ds"][rows, :]
        blt = bl2[:, at]
        for c in range(CH):
            if c < NX:
                red = jnp.sum(jnp.concatenate(halves[c], axis=0) * rr[c:c + 1, :], axis=1, keepdims=True)
            else:
                xc = jnp.concatenate(halves[c], axis=0)
                xh = xc.astype(BF16)
                xo = (xc - xh.astype(F32)).astype(BF16)
                red = dot(jnp.concatenate([xh, xo], axis=1), rdup, NT)
            blt = jnp.where(lanes64 == base + c, red, blt)
        bl2[:, at] = blt
        slot = lax.rem(t, 2)
        for c in range(CH):
            w["br8"][slot, c * 8:c * 8 + 8, :] = br[c]
        tot = w["br8"][slot, pl.ds(0, 8, stride=8), :]
        for z in range(1, 8):
            tot = tot + w["br8"][slot, pl.ds(z, 8, stride=8), :]
        w["br2"][pl.ds(pl.multiple_of(block * 128 + t * 8, 8), 8), :] = tot

    ev = w["e"][...].reshape(16 * I, J)
    hi = ev.astype(BF16)
    lo = (ev - hi.astype(F32)).astype(BF16)
    kt = w["k2"][at, :]
    bqw = dot(jnp.concatenate([hi, lo], axis=1), jnp.concatenate([kt, kt], axis=1), NT)
    tot = jnp.zeros((I, 128), F32)
    lane2 = lax.broadcasted_iota(jnp.int32, (I, 128), 1)
    for t in range(16):
        tot = jnp.where((lane2 >> 3) == t, bqw[t * I:(t + 1) * I, :], tot)
    bq2[:, at] = f * tot
    sub_r = lax.broadcasted_iota(jnp.int32, (32, 256), 0)
    sub_c = lax.broadcasted_iota(jnp.int32, (32, 256), 1)
    keep = jnp.where((sub_r >> 3) == (sub_c >> 6), 1.0, 0.0).astype(BF16)
    for u in range(4):
        qrow = w["qt"][pl.ds(pl.multiple_of(n * 128 + u * 32, 32), 32), :]
        lhs = jnp.concatenate([qrow, qrow], axis=1) * keep
        part = dot(jnp.concatenate([lhs, lhs], axis=1), jnp.concatenate([hi[u * 256:u * 256 + 256], lo[u * 256:u * 256 + 256]], axis=0))
        w["bk2"][pl.ds(pl.multiple_of(block * 128 + u * 32, 32), 32), :] = f * part


def greet(groups):
    barrier = pltpu.get_barrier_semaphore()
    for axis, n in groups:
        me = lax.axis_index(axis)

        @pl.loop(1, n)
        def _(s):
            pl.semaphore_signal(barrier, inc=1, device_id={axis: lax.rem(me + s, n)}, device_id_type=MESH)


class Trade:
    def __init__(self, axis, n, src, dst, send_sem, recv_sem):
        self.axis, self.n, self.src, self.dst, self.send_sem, self.recv_sem = axis, n, src, dst, send_sem, recv_sem
        self.me = lax.axis_index(axis)

    def copy(self, s):
        peer = lax.rem(self.me + s, self.n)
        return pltpu.make_async_remote_copy(
            src_ref=self.src(peer), dst_ref=self.dst(self.me), send_sem=self.send_sem.at[s], recv_sem=self.recv_sem.at[s],
            device_id={self.axis: peer}, device_id_type=MESH)

    def start(self):
        @pl.loop(1, self.n)
        def _(s):
            self.copy(s).start()

    def finish(self):
        @pl.loop(1, self.n)
        def _(s):
            self.copy(s).wait_recv()

    def drain(self):
        @pl.loop(1, self.n)
        def _(s):
            self.copy(s).wait_send()


def to_pairs(wide, stage, count, pad=0):
    for i in range(32):
        for z in range(2):
            at = (i % 2) * 256 + z * 128
            piece = wide[z, pl.ds(i, count, stride=32), :]
            if pad:
                piece = jnp.concatenate([piece, jnp.zeros((pad, 128), F32)], axis=0)
            stage[i // 2, :, at:at + 128] = piece.astype(BF16)


def from_pairs(recv, wide, count):
    for i in range(32):
        for z in range(2):
            at = (i % 2) * 256 + z * 128
            wide[z, pl.ds(i, count, stride=32), :] = recv[i // 2, :, at:at + 128][:count].astype(F32)


def layer(names, x, u, wq, wk, wl, wr, wf, allowance, fac, grads, gq, gk, gl, gr, go, *scratch):
    w = dict(zip(names, scratch))
    me, row = lax.axis_index("head"), lax.axis_index("row")
    jb = lax.rem(row, 2)
    partner, pj = row + 1 - 2 * jb, 1 - jb
    other = pl.ds(pl.multiple_of(pj * 32, 32), 32)
    own = pl.ds(pl.multiple_of(jb * 32, 32), 32)
    hs, rs, ps = w["hs"], w["rs"], w["ps"]

    def half(j):
        return pl.ds(pl.multiple_of(j * 128, 128), 128)

    def over_head(n, src, dst):
        return Trade("head", HEADS, src, dst, hs.at[2 * n], hs.at[2 * n + 1])

    def over_row(n, src, dst):
        return Trade("row", ROWS, src, dst, rs.at[2 * n], rs.at[2 * n + 1])

    def to_partner(n, src, dst):
        return pltpu.make_async_remote_copy(src_ref=src, dst_ref=dst, send_sem=ps.at[0, n], recv_sem=ps.at[1, n],
                                            device_id={"row": partner}, device_id_type=MESH)

    greet([("head", HEADS), ("row", ROWS)])
    wself, wall, wide = w["wself"], w["wall"], w["wide"]
    wself[...] = jnp.concatenate([wk[...], wr[...], wq[...], wl[...], wf[...], jnp.zeros((8, 128), BF16)], axis=0)
    for z in range(2):
        wide[z, 0:256, :] = x[:, :, z * 128:z * 128 + 128].reshape(256, 128).astype(F32)
        wide[z, 256:512, :] = u[:, :, z * 128:z * 128 + 128].reshape(256, 128).astype(F32)
    to_pairs(wide, w["stage1"], 16)
    pl.semaphore_wait(pltpu.get_barrier_semaphore(), HEADS + ROWS - 2)
    inputs = over_head(0, lambda p: w["stage1"].at[p], lambda p: w["recv1"].at[p])
    weights = over_head(1, lambda p: wself, lambda p: wall.at[p])
    weights.start()
    inputs.start()
    w["recv1"][me] = w["stage1"][me]
    wall[me] = wself[...]
    constants(w)
    node = row * 32 + lax.broadcasted_iota(jnp.int32, (32, 256), 0)
    valid = (allowance[...] == 1) | (node == lax.broadcasted_iota(jnp.int32, (32, 256), 1))
    w["bias"][...] = jnp.where(valid, 0.0, -1e30).astype(BF16)
    bias_out = to_partner(0, w["bias"], w["ql"].at[jb, 16])
    bias_out.start()
    w["ql"][jb, 16] = w["bias"][...]
    inputs.finish()
    both = w["recv1"][...].astype(F32)
    w["xp"][...] = both[:, 0:8].reshape(128, 512).astype(BF16)
    w["up"][...] = both[:, 8:16].reshape(128, 512).astype(BF16)
    weights.finish()

    mapped = over_head(2, lambda p: w["stage2"].at[p], lambda p: w["recv2"].at[p])
    for first in range(0, HEADS, 4):
        peers = [lax.rem(me + first + a, HEADS) for a in range(4)]
        of_x = dot(jnp.concatenate([wall[p, 0:32] for p in peers], axis=0), w["xp"][...]).astype(BF16)
        of_u = dot(jnp.concatenate([wall[p, 32:48] for p in peers], axis=0), w["up"][...]).astype(BF16)
        for a, p in enumerate(peers):
            w["stage2"][p, 0:32] = of_x[a * 32:a * 32 + 32]
            w["stage2"][p, 32:48] = of_u[a * 16:a * 16 + 16]
            if first + a:
                mapped.copy(first + a).start()
            else:
                w["recv2"][me] = w["stage2"][me]
    mapped.finish()
    from_pairs(w["recv2"], wide, 40)
    nat = w["nat"]
    for z in range(2):
        nat[:, :, z * 128:z * 128 + 128] = wide[z, 0:1280, :].astype(BF16).reshape(40, 32, 128)

    ql, kr, gg = w["ql"], w["kr"], w["gg"]
    pairs_in = over_row(0, lambda p: nat.at[pl.ds(0, 16), :, half(lax.rem(p, 2))], lambda p: kr.at[p])
    ahead = [to_partner(1, nat.at[pl.ds(16, 16)], ql.at[jb, pl.ds(0, 16)]),
             to_partner(2, nat.at[pl.ds(32, 8), :, half(pj)], gg.at[jb])]
    pairs_in.start()
    for copy in ahead:
        copy.start()
    ql[jb, 0:16] = nat[16:32]
    gg[jb] = nat[32:40, :, half(jb)]
    kr[row] = nat[0:16, :, half(jb)]
    bias_out.wait()
    for copy in ahead:
        copy.wait()
    pairs_in.finish()

    f = fac[0]
    scores(ql, kr, w)
    forward(gg, f, w["mx"], w)
    mixed_out = to_partner(3, w["mx"].at[:, other], w["mixin"])
    mixed_out.start()
    ql2, qlin, kro, krin = w["ql2"], w["qlin"], w["kro"], w["krin"]
    pairs_out = over_row(1, lambda p: kro.at[p], lambda p: krin.at[p])
    mixed = over_head(3, lambda p: w["stagem"].at[p], lambda p: w["recvm"].at[p])

    def block_out(k, z):
        part = pl.ds(pl.multiple_of(z * 256, 256), 256)
        return to_partner(4 + k, ql2.at[:, other, part], qlin.at[:, :, part])

    @pl.loop(0, ROWS)
    def _(k):
        z = lax.rem(row + 1 + k, ROWS)

        @pl.loop(0, 2)
        def _(block):
            backward(2 * z + block, block, f, ql2.at[0], ql2.at[1], w)

        for c in range(CH):
            kro[z, c] = w["bk2"][pl.ds(c, 32, stride=8), :]
            kro[z, CH + c] = w["br2"][pl.ds(c, 32, stride=8), :]
        block_out(k, z).start()

        @pl.when(k < ROWS - 1)
        def _():
            pairs_out.copy(k + 1).start()

        @pl.when(k == ROWS - 1)
        def _():
            krin[row] = kro[row]

        @pl.when(k == 0)
        def _():
            mixed_out.wait()
            mixf = w["mixf"]
            for c in range(CH):
                mixf[jb, c * 32:c * 32 + 32, :] = w["mx"][c, own, :].astype(F32)
                mixf[pj, c * 32:c * 32 + 32, :] = w["mixin"][c].astype(F32)
            to_pairs(mixf, w["stagem"], 8, 8)
            mixed.start()
            w["recvm"][me] = w["stagem"][me]

    @pl.loop(0, ROWS)
    def _(k):
        block_out(k, lax.rem(row + 1 + k, ROWS)).wait()

    total = (ql2[:, own, :] + qlin[...]).astype(BF16).reshape(64, 2048)
    for h in range(2):
        plain = dot(total[:, h * 1024:h * 1024 + 1024], w["pt"][...])
        for c in range(CH):
            wide[h, 512 + c * 32:544 + c * 32, :] = plain[0:32, c * 128:c * 128 + 128]
            wide[h, 768 + c * 32:800 + c * 32, :] = plain[32:64, c * 128:c * 128 + 128]
    mixed.finish()
    gu = dot(w["recvm"][...].reshape(256, 512), w["up"][...], NT).reshape(16, 16, 128)
    gws = w["gws"]
    gws[:, 32:40, :] = gu[:, 0:8]
    pairs_out.finish()
    for j in range(2):
        total = krin[j] + krin[2 + j] + krin[4 + j] + krin[6 + j]
        wide[j, 0:512, :] = total.reshape(512, 128)
    to_pairs(wide, w["stage3"], 32)
    backs = over_head(4, lambda p: w["stage3"].at[p], lambda p: w["recv3"].at[p])
    backs.start()
    w["recv3"][me] = w["stage3"][me]
    backs.finish()

    every = w["recv3"][...].reshape(512, 512)
    gws[:, 0:32, :] = dot(every, w["xp"][...], NT).reshape(16, 32, 128)
    sums = over_head(5, lambda p: gws.at[p], lambda p: w["gwin"].at[p])
    sums.start()
    w["gwin"][me] = gws[me]
    image = dot(wall[:, 0:32, :].reshape(512, 128), every, TN).reshape(16, 8, 512)
    w["stage4"][...] = jnp.concatenate([image, jnp.zeros((16, 8, 512), F32)], axis=1).astype(BF16)
    images = over_head(6, lambda p: w["stage4"].at[p], lambda p: w["recv4"].at[p])
    images.start()
    w["recv4"][me] = w["stage4"][me]
    sums.finish()
    total = w["gwin"][0]
    for p in range(1, HEADS):
        total = total + w["gwin"][p]
    w["part"][...] = total
    last = over_row(2, lambda p: w["part"], lambda p: w["gwrow"].at[p])
    last.start()
    w["gwrow"][row] = total
    images.finish()
    from_pairs(w["recv4"], wide, 8)
    for z in range(2):
        grads[:, :, z * 128:z * 128 + 128] = wide[z, 0:256, :].astype(BF16).reshape(8, 32, 128)
    last.finish()
    total = w["gwrow"][0]
    for p in range(1, ROWS):
        total = total + w["gwrow"][p]
    total = total * (1.0 / 256.0)
    for n, out in enumerate((gk, gr, gq, gl, go)):
        out[...] = total[8 * n:8 * n + 8]
    for trade in (inputs, weights, mapped, pairs_in, pairs_out, mixed, backs, sums, images, last):
        trade.drain()


def layer_scratch():
    vmem, dma = pltpu.VMEM, pltpu.SemaphoreType.DMA
    return dict(
        core_scratch(),
        wide=vmem((2, 1280, 128), F32), wself=vmem((48, 128), BF16), wall=vmem((16, 48, 128), BF16),
        stage1=vmem((16, 16, 512), BF16), recv1=vmem((16, 16, 512), BF16), xp=vmem((128, 512), BF16), up=vmem((128, 512), BF16),
        stage2=vmem((16, 48, 512), BF16), recv2=vmem((16, 48, 512), BF16), nat=vmem((40, 32, 256), BF16), bias=vmem((32, 256), BF16),
        ql=vmem((2, 17, 32, 256), BF16), kr=vmem((8, 16, 32, 128), BF16), gg=vmem((2, 8, 32, 128), BF16),
        ql2=vmem((2, 64, 2048), F32), qlin=vmem((2, 32, 2048), F32), kro=vmem((8, 16, 32, 128), F32), krin=vmem((8, 16, 32, 128), F32),
        mx=vmem((8, 64, 128), BF16), mixin=vmem((8, 32, 128), BF16), mixf=vmem((2, 256, 128), F32),
        stagem=vmem((16, 16, 512), BF16), recvm=vmem((16, 16, 512), BF16),
        stage3=vmem((16, 32, 512), BF16), recv3=vmem((16, 32, 512), BF16), stage4=vmem((16, 16, 512), BF16), recv4=vmem((16, 16, 512), BF16),
        gws=vmem((16, 40, 128), F32), gwin=vmem((16, 40, 128), F32), part=vmem((40, 128), F32), gwrow=vmem((8, 40, 128), F32),
        hs=dma((14, 16)), rs=dma((6, 8)), ps=dma((2, 12)),
    )


def local(x, allowance, asking, lookup, first_content, second_content, final, scaling, upstream):
    vm = pl.BlockSpec(memory_space=pltpu.VMEM)
    names = layer_scratch()
    grads, gq, gk, gl, gr, go = pl.pallas_call(
        functools.partial(layer, list(names)),
        out_shape=[jax.ShapeDtypeStruct((8, 32, 256), BF16)] + [jax.ShapeDtypeStruct((8, 128), F32)] * 5,
        in_specs=[vm] * 8 + [pl.BlockSpec(memory_space=pltpu.SMEM)], out_specs=[vm] * 6,
        scratch_shapes=list(names.values()),
        compiler_params=pltpu.CompilerParams(collective_id=0, has_side_effects=True, vmem_limit_bytes=56 * 2 ** 20),
        name="layer",
    )(x, upstream, asking.T, lookup.T, first_content.T, second_content.T, final, allowance, scaling)
    return grads, gq.T, gk.T, gl.T, gr.T, go


def solution(mesh):
    pairs, columns = P("head", "row", None), P(None, "head")
    placed = (pairs, P("row", None), columns, columns, columns, columns, P("head", None), P("head"), pairs)
    return jax.shard_map(
        local, mesh=mesh, in_specs=placed,
        out_specs=(pairs, columns, columns, columns, columns, P("head", None)), check_vma=False,
    )
```

time: 215 us -> 160 us (0.74)
  Pallas kernels: 203 us -> 153 us
  local copies, waits for them, and re-layouts: 8 us -> 4.88 us
    pallas_call x3 -> x1, Pallas kernels: 203 us -> 153 us  [local(): pl.pallas_call(functools.partial(layer, list(names)), out_shape=[jax.Shap...]
    unnamed x7 -> x16, local copies, waits for them, and re-layouts: 1.27 us -> 4.88 us
    squeeze x4 -> x0, local copies, waits for them, and re-layouts: 2.73 us -> none  [local(): return (grads, of_x[2].T, of_x[0].T, of_x[3].T, of_x[1].T, of_u)]
where the time goes in v2:
time: 160 us
  Pallas kernels  153 us (96%)
  local copies, waits for them, and re-layouts  4.88 us (3%)
    pallas_call x1, Pallas kernels, local(): pl.pallas_call(functools.partial(layer, list(names)), out_shape=[jax.Shap...  153 us
    unnamed x16, local copies, waits for them, and re-layouts  4.88 us

profile of v2, /device:TPU:1, one launch (start us, length us, event | category | flops | bytes accessed | tf_op | source)
XLA Modules:
  0.0 159.7 jit_solution(1685724484184826585)
XLA Ops:
  1.3 153.5 %layer.1 = (bf16[8,32,256]{2,1,0:T(8,128)(2,1)}, f32[8,128]{1,0:T(8,128)}, f32[8,128]{1,0:T(8,128)}, f32[8,128]{1,0:T(8,128)}, f32[8,128]{1,0:T(8,128)}, /*index=5*/f32[8,128]{1,0:T(8,128)}) custom-call(bf16[8,32,256]{2,1,0:T(8,128)(2,1)} %x.1, bf16[8,32,256]{2,1,0:T(8,128)(2,1)} %u.1, bf16[8,128]{1,0:T(8,128)(2,1)} %bitcast.12, bf16[8,128]{1,0:T(8,128)(2,1)} %bitcast.13, ...), custom_call_target="tpu_custom_call" | custom-call | tf_op jit(solution)/shard_map/layer/pallas_call | solution.py:454
  154.8 0.0 copy-start.4
  154.8 1.6 copy.22
  156.4 0.0 copy-done.4
  156.4 0.0 copy-start.3
  156.4 0.6 copy.23
  157.0 0.1 copy-done.3
  157.0 0.0 copy-start.2
  157.0 0.6 copy.24
  157.6 0.1 copy-done.2
  157.7 0.0 copy-start.1
  157.7 0.6 copy.25
  158.3 0.1 copy-done.1
  158.4 0.0 copy-start
  158.4 0.6 copy.26
  159.0 0.1 copy-done
  159.1 0.6 copy.27
Async XLA Ops:
  154.8 1.6 copy-start.4
  156.4 0.7 copy-start.3
  157.0 0.7 copy-start.2
  157.7 0.7 copy-start.1
  158.4 0.7 copy-start

commit v3 on v2

v3 whole, which is shorter than its diff:
```python
import functools

import jax
import jax.numpy as jnp
from jax import lax
from jax.experimental import pallas as pl
from jax.experimental.pallas import tpu as pltpu
from jax.sharding import PartitionSpec as P

F32, BF16 = jnp.float32, jnp.bfloat16
MESH = pl.DeviceIdType.MESH
NT = (((1,), (1,)), ((), ()))
NN = (((1,), (0,)), ((), ()))
TN = (((0,), (0,)), ((), ()))
CH, I, L, J = 8, 64, 256, 128
HEADS, ROWS = 16, 8


def dot(a, b, dims=NN):
    return lax.dot_general(a, b, dims, preferred_element_type=F32)


def core_scratch():
    return dict(
        pt=pltpu.VMEM((1024, 1024), BF16),
        q2=pltpu.VMEM((I, 2048), BF16), b2=pltpu.VMEM((I, 2048), BF16),
        qt=pltpu.VMEM((2048, 128), BF16), kf=pltpu.VMEM((2048, J), F32), rf=pltpu.VMEM((2048, J), F32),
        k2=pltpu.VMEM((2048, J), BF16), mt=pltpu.VMEM((16, 256), BF16), wc=pltpu.VMEM((128, 1024), BF16), lb16=pltpu.VMEM((I, 2048), BF16),
        s=pltpu.VMEM((L, I, J), F32), m=pltpu.VMEM((I, J), F32), gs=pltpu.VMEM((CH, I, J), F32), ds=pltpu.VMEM((I, J), F32),

        e=pltpu.VMEM((16, I, J), F32), br8=pltpu.VMEM((2, 64, J), F32),
    )


def permutation(pt):
    @pl.loop(0, 8)
    def _(n):
        a = lax.broadcasted_iota(jnp.int32, (128, 1024), 0) + n * 128
        b = lax.broadcasted_iota(jnp.int32, (128, 1024), 1)
        hit = ((a >> 3) == (b & 127)) & ((a & 7) == (b >> 7))
        pt[pl.ds(pl.multiple_of(n * 128, 128), 128), :] = jnp.where(hit, 1.0, 0.0).astype(BF16)


def constants(w):
    permutation(w["pt"])
    row = lax.broadcasted_iota(jnp.int32, (16, 256), 0)
    lane = lax.broadcasted_iota(jnp.int32, (16, 256), 1)
    w["mt"][...] = jnp.where(((lane & 127) >> 3) == row, 1.0, 0.0).astype(BF16)
    ra = lax.broadcasted_iota(jnp.int32, (128, 1024), 0)
    rb_ = lax.broadcasted_iota(jnp.int32, (128, 1024), 1)
    w["wc"][...] = jnp.where((ra & 7) == (rb_ >> 7), 1.0, 0.0).astype(BF16)


def prepare(wide, w):
    pt = w["pt"]
    for half in range(2):
        out = slice(half * 1024, half * 1024 + 1024)
        qcat = jnp.concatenate([wide[half, c * I:c * I + I, :] for c in range(CH)], axis=1).astype(BF16)
        lcat = jnp.concatenate([wide[half, c * I:c * I + I, :] for c in range(CH, 2 * CH)], axis=1).astype(BF16)
        bcat = jnp.concatenate([wide[half, 24 * I:25 * I, :].astype(BF16), jnp.zeros((I, 896), BF16)], axis=1)
        got = dot(jnp.concatenate([qcat, lcat, bcat], axis=0), pt[...], NT)
        w["q2"][:, out] = got[:I].astype(BF16)
        w["lb16"][:, out] = got[I:2 * I].astype(BF16)
        w["b2"][:, out] = got[2 * I:].astype(BF16)
        w["qt"][out, :] = dot(pt[...], jnp.concatenate([qcat, qcat], axis=0), NT).astype(BF16)
    w["m"][...] = jnp.full((I, J), -3e38, F32)


def scores(n, w):
    at = pl.ds(pl.multiple_of(n * 128, 128), 128)
    k2 = w["kf"][at, :].astype(BF16)
    w["k2"][at, :] = k2
    qb = jnp.concatenate([w["q2"][:, at], w["b2"][:, at]], axis=1)
    kk = jnp.concatenate([k2, jnp.ones((128, J), BF16)], axis=0)
    lhs = jnp.concatenate([qb * w["mt"][t:t + 1, :] for t in range(16)], axis=0)
    raw = dot(lhs, kk).reshape(16, I, J)
    top = w["m"][...]
    for t in range(16):
        top = jnp.maximum(top, raw[t])
    w["m"][...] = top
    w["s"][pl.ds(n * 16, 16)] = raw


def forward(wide, mine, f, mixed, w):
    @pl.loop(0, 4)
    def _(ip):
        rows = pl.ds(pl.multiple_of(ip * 16, 16), 16)
        top = w["m"][rows, :]

        def step(n, carry):
            total, acc = carry
            acc = list(acc)
            tile = w["lb16"][rows, pl.ds(pl.multiple_of(n * 128, 128), 128)]
            lhs = jnp.concatenate([tile * w["mt"][t:t + 1, :128] for t in range(16)], axis=0)
            spread = dot(lhs, w["wc"][...])
            for t in range(16):
                lv = n * 16 + t
                wt = jnp.exp(f * (w["s"][lv, rows, :] - top))
                w["s"][lv, rows, :] = wt
                total = total + wt
                rr = w["rf"][pl.ds(pl.multiple_of(lv * 8, 8), 8), :]
                for c in range(CH):
                    lb = spread[t * 16:t * 16 + 16, c * 128:c * 128 + 128]
                    acc[c] = acc[c] + (wt * rr[c:c + 1, :]) * lb
            return total, tuple(acc)

        zero = jnp.zeros((16, J), F32)
        total, acc = lax.fori_loop(0, 16, step, (zero, (zero,) * CH))
        inv = 1.0 / total
        delta = zero
        for c in range(CH):
            gc = wide[mine, pl.ds(pl.multiple_of((16 + c) * I + ip * 16, 16), 16), :]
            mc = acc[c] * inv
            mixed[c, rows, :] = mc.astype(BF16)
            delta = delta + gc * mc
            w["gs"][c, rows, :] = gc * inv
        w["ds"][rows, :] = delta * inv


def backward(n, chip, place, f, bq2, bl2, kro, w):
    at = pl.ds(pl.multiple_of(n * 128, 128), 128)
    bl2[:, at] = jnp.zeros((I, 128), F32)

    @pl.loop(0, 16, unroll=4)
    def _(t):
        lv = n * 16 + t
        lanes64 = lax.broadcasted_iota(jnp.int32, (I, 128), 1)
        pick = jnp.where((lanes64 >> 3) == t, 1.0, 0.0).astype(BF16)
        spread = dot(w["lb16"][:, at] * pick, w["wc"][...])
        rr = w["rf"][pl.ds(pl.multiple_of(lv * 8, 8), 8), :]
        rb = [jnp.broadcast_to(rr[c:c + 1, :], (8, J)) for c in range(CH)]
        br = [jnp.zeros((8, J), F32) for c in range(CH)]
        base = t * 8
        halves = [[] for c in range(CH)]
        for it in range(8):
            rows = slice(it * 8, it * 8 + 8)
            wt = w["s"][lv, rows, :]
            pgp = None
            for c in range(CH):
                x = wt * w["gs"][c, rows, :]
                xl = x * spread[rows, c * 128:c * 128 + 128]
                br[c] = br[c] + xl
                term = xl * rb[c]
                pgp = term if pgp is None else pgp + term
                halves[c].append(x)
            w["e"][t, rows, :] = pgp - wt * w["ds"][rows, :]
        blt = bl2[:, at]
        for c in range(CH):
            red = jnp.sum(jnp.concatenate(halves[c], axis=0) * rr[c:c + 1, :], axis=1, keepdims=True)
            blt = jnp.where(lanes64 == base + c, red, blt)
        bl2[:, at] = blt
        slot = lax.rem(t, 2)
        for c in range(CH):
            w["br8"][slot, c * 8:c * 8 + 8, :] = br[c]
        tot = w["br8"][slot, pl.ds(0, 8, stride=8), :]
        for z in range(1, 8):
            tot = tot + w["br8"][slot, pl.ds(z, 8, stride=8), :]
        kro[2 * chip + lax.rem(t // 2, 2), place + (t // 4) * 4 + lax.rem(t, 2), 8:16, :] = tot

    ev = w["e"][...].reshape(16 * I, J)
    hi = ev.astype(BF16)
    lo = (ev - hi.astype(F32)).astype(BF16)
    kt = w["k2"][at, :]
    bqw = dot(jnp.concatenate([hi, lo], axis=1), jnp.concatenate([kt, kt], axis=1), NT)
    tot = jnp.zeros((I, 128), F32)
    lane2 = lax.broadcasted_iota(jnp.int32, (I, 128), 1)
    for t in range(16):
        tot = jnp.where((lane2 >> 3) == t, bqw[t * I:(t + 1) * I, :], tot)
    bq2[:, at] = f * tot
    sub_r = lax.broadcasted_iota(jnp.int32, (32, 256), 0)
    sub_c = lax.broadcasted_iota(jnp.int32, (32, 256), 1)
    keep = jnp.where((sub_r >> 3) == (sub_c >> 6), 1.0, 0.0).astype(BF16)
    for u in range(4):
        qrow = w["qt"][pl.ds(pl.multiple_of(n * 128 + u * 32, 32), 32), :]
        lhs = jnp.concatenate([qrow, qrow], axis=1) * keep
        part = dot(jnp.concatenate([lhs, lhs], axis=1), jnp.concatenate([hi[u * 256:u * 256 + 256], lo[u * 256:u * 256 + 256]], axis=0))
        part = f * part
        for core in range(2):
            for a in range(2):
                first = (core * 2 + a) * 8
                kro[2 * chip + core, place + u * 4 + a, 0:8, :] = part[first:first + 8]


def greet(groups):
    barrier = pltpu.get_barrier_semaphore()
    for n, peer in groups:
        @pl.loop(1, n)
        def _(s):
            pl.semaphore_signal(barrier, inc=1, device_id=peer(s), device_id_type=MESH)


class Trade:
    def __init__(self, n, peer, src, dst, send_sem, recv_sem):
        self.n, self.peer, self.src, self.dst, self.send_sem, self.recv_sem = n, peer, src, dst, send_sem, recv_sem

    def copy(self, s):
        return pltpu.make_async_remote_copy(
            src_ref=self.src(s), dst_ref=self.dst, send_sem=self.send_sem.at[s], recv_sem=self.recv_sem.at[s],
            device_id=self.peer(s), device_id_type=MESH)

    def start(self):
        @pl.loop(1, self.n)
        def _(s):
            self.copy(s).start()

    def finish(self):
        @pl.loop(1, self.n)
        def _(s):
            self.copy(s).wait_recv()

    def drain(self):
        @pl.loop(1, self.n)
        def _(s):
            self.copy(s).wait_send()


def lane_of(i, z):
    return z * 256 + (i % 2) * 128


def to_pairs(wide, stage, count, rows, first=0):
    for i in range(32):
        for z in range(2):
            at = lane_of(i, z)
            piece = wide[z, pl.ds(i, count, stride=32), :]
            if count % 16:
                piece = jnp.concatenate([piece, jnp.zeros((16 - count % 16, 128), F32)], axis=0)
            stage[i // 2, first:first + rows, at:at + 128] = piece.astype(BF16)


def from_pairs(recv, lo, hi, wide, offset, stride):
    for i in range(32):
        for z in range(2):
            at = lane_of(i, z)
            wide[z, pl.ds(offset + i, hi - lo, stride=stride), :] = recv[i // 2, lo:hi, at:at + 128].astype(F32)


def layer(names, x, u, wq, wk, wl, wr, wf, allowance, fac, grads, gq, gk, gl, gr, go, *scratch):
    w = dict(zip(names, scratch))
    me, row = lax.axis_index("head"), lax.axis_index("row")
    core = lax.rem(me, 2)
    x_hi, x_lo, y_lo = lax.rem(row // 2, 2), lax.rem(row, 2), row // 4
    slot = (me // 2) * 2 + x_hi
    part = y_lo * 4 + x_lo * 2 + core
    block = part // 2

    def head_peer(s):
        return {"head": lax.rem(me + s, HEADS), "row": row}

    def row_peer(s):
        return {"head": me, "row": lax.rem(row + s, ROWS)}

    def slot_at(s):
        return lax.rem(slot // 4 + s // 4, 4) * 4 + lax.rem(slot + s, 4)

    def slot_peer(s):
        to = slot_at(s)
        return {"head": (to // 2) * 2 + core, "row": y_lo * 4 + lax.rem(to, 2) * 2 + x_lo}

    def part_peer(s):
        to = lax.rem(part + s, 8)
        return {"head": (me // 2) * 2 + lax.rem(to, 2), "row": (to // 4) * 4 + x_hi * 2 + lax.rem(to // 2, 2)}

    partner = {"head": me + 1 - 2 * core, "row": row}
    hs, rs, ps = w["hs"], w["rs"], w["ps"]

    def over(n, size, peer, src, dst):
        sems = hs if size == HEADS else rs
        return Trade(size, peer, src, dst, sems.at[2 * n], sems.at[2 * n + 1])

    def to_partner(n, src, dst):
        return pltpu.make_async_remote_copy(src_ref=src, dst_ref=dst, send_sem=ps.at[0, n], recv_sem=ps.at[1, n],
                                            device_id=partner, device_id_type=MESH)

    def head_at(s):
        return lax.rem(me + s, HEADS)

    greet([(HEADS, head_peer), (ROWS, row_peer), (HEADS, slot_peer), (8, part_peer)])
    wself, wall, wide = w["wself"], w["wall"], w["wide"]
    f0 = jnp.full((8, 128), fac[0], F32)
    f1 = f0 - f0.astype(BF16).astype(F32)
    f2 = f1 - f1.astype(BF16).astype(F32)
    tile = lax.broadcasted_iota(jnp.int32, (8, 128), 0)
    factor = jnp.where(tile == 0, f0, jnp.where(tile == 1, f1, jnp.where(tile == 2, f2, 0.0)))
    wself[...] = jnp.concatenate([wk[...], wr[...], wq[...], wl[...], wf[...], factor.astype(BF16)], axis=0)
    for z in range(2):
        wide[z, 0:256, :] = x[:, :, z * 128:z * 128 + 128].reshape(256, 128).astype(F32)
        wide[z, 256:512, :] = u[:, :, z * 128:z * 128 + 128].reshape(256, 128).astype(F32)
    to_pairs(wide, w["stage1"], 16, 16)
    pl.semaphore_wait(pltpu.get_barrier_semaphore(), 2 * HEADS + ROWS + 8 - 4)
    inputs = over(0, HEADS, head_peer, lambda s: w["stage1"].at[head_at(s)], w["recv1"].at[me])
    weights = over(1, HEADS, head_peer, lambda s: wself, wall.at[me])
    weights.start()
    inputs.start()
    w["recv1"][me] = w["stage1"][me]
    wall[me] = wself[...]
    constants(w)
    node = row * 32 + lax.broadcasted_iota(jnp.int32, (32, 128), 0)
    column = lax.broadcasted_iota(jnp.int32, (32, 128), 1)
    for z in range(2):
        valid = (allowance[:, z * 128:z * 128 + 128] == 1) | (node == column + z * 128)
        w["mask"][z] = jnp.where(valid, 0.0, -1e30)
    bias = jnp.concatenate([w["mask"][z, pl.ds(2 * me + a, 1), :] for z in range(2) for a in range(2)], axis=1)
    bias = jnp.broadcast_to(bias, (8, 512))
    inputs.finish()
    both = w["recv1"][...].astype(F32)
    w["xp"][...] = both[:, 0:8].reshape(128, 512).astype(BF16)
    w["up"][...] = both[:, 8:16].reshape(128, 512).astype(BF16)
    weights.finish()

    stage2, recv2, kr = w["stage2"], w["recv2"], w["kr"]
    mapped = over(2, HEADS, slot_peer, lambda s: stage2.at[slot_at(s)], recv2.at[slot])
    for first in range(0, HEADS, 4):
        peers = [slot_at(first + a) for a in range(4)]
        of_x = dot(jnp.concatenate([wall[p, 0:32] for p in peers], axis=0), w["xp"][...]).astype(BF16)
        of_u = dot(jnp.concatenate([wall[p, 32:48] for p in peers], axis=0), w["up"][...])
        for a, p in enumerate(peers):
            stage2[p, 0:32] = of_x[a * 32:a * 32 + 32]
            stage2[p, 32:48] = jnp.concatenate([of_u[a * 16:a * 16 + 8], bias], axis=0).astype(BF16)
            if first + a:
                mapped.copy(first + a).start()
            else:
                recv2[slot] = stage2[slot]

    def kr_copy(g, s):
        four = pl.ds(lax.rem(slot // 4 + 4 - g, 4) * 4, 4)
        to = lax.rem(part + s, 8)
        return pltpu.make_async_remote_copy(
            src_ref=recv2.at[four, pl.ds(0, 16), pl.ds(pl.multiple_of(lax.rem(to, 2) * 256, 128), 256)], dst_ref=kr.at[part, four],
            send_sem=w["ks"].at[0, g, s], recv_sem=w["ks"].at[1, g, s], device_id=part_peer(s), device_id_type=MESH)

    def near_copy(g):
        four = pl.ds(lax.rem(slot // 4 + 4 - g, 4) * 4, 4)
        return to_partner(g, recv2.at[four, pl.ds(16, 32)], w["near"].at[four])

    @pl.loop(0, 4)
    def _(g):
        @pl.loop(0, 4)
        def _(a):
            @pl.when(g * 4 + a > 0)
            def _():
                mapped.copy(g * 4 + a).wait_recv()

        near_copy(g).start()

        @pl.loop(1, 8)
        def _(s):
            kr_copy(g, s).start()

    near = w["near"]
    wide2 = w["wide2"]
    own = pl.multiple_of(core * 32, 32)
    from_pairs(recv2, 16, 48, wide2, core * 32, I)

    @pl.loop(0, 4)
    def _(g):
        near_copy(g).wait_recv()

    from_pairs(near, 0, 32, wide2, 32 - core * 32, I)
    prepare(wide2, w)

    f = jnp.sum(wall[slot, 32:48].astype(F32)[8:16], axis=0, keepdims=True)

    def groups(chip):
        for hi in range(2):
            for y in range(2):
                yield 2 * ((chip // 2) * 4 + hi * 2 + lax.rem(chip, 2)) + y, y * 8 + hi

    @pl.loop(0, 4)
    def _(k):
        chip = lax.rem(block + 4 - k, 4)
        for c in range(2):
            @pl.when(2 * chip + c != part)
            def _():
                @pl.loop(0, 4)
                def _(g):
                    kr_copy(g, lax.rem(part + 8 - 2 * chip - c, 8)).wait_recv()

            @pl.when(2 * chip + c == part)
            def _():
                kr[part] = recv2[:, 0:16, pl.ds(pl.multiple_of(core * 256, 128), 256)]

        for n, first in groups(chip):
            for t in range(16):
                at = (first + (t // 4) * 2)
                tile = kr[2 * chip + (t // 2) % 2, at, :, (t % 2) * 128:(t % 2) * 128 + 128].astype(F32)
                rows = pl.ds(pl.multiple_of(n * 128 + t * 8, 8), 8)
                w["kf"][rows, :] = tile[0:8]
                w["rf"][rows, :] = tile[8:16]
            scores(n, w)

    forward(wide2, core, f, w["mx"], w)
    mine, other = pl.ds(own, 32), pl.ds(pl.multiple_of(32 - core * 32, 32), 32)
    mixed_out = to_partner(4, w["mx"].at[:, other], w["mixin"])
    mixed_out.start()
    ql2, qlin, kro, krin = w["ql2"], w["qlin"], w["kro"], w["krin"]
    pairs_out = over(0, 8, part_peer, lambda s: kro.at[lax.rem(part + s, 8)], krin.at[part])
    mixed = over(3, HEADS, slot_peer, lambda s: w["stagem"].at[slot_at(s)], w["recvm"].at[slot])

    def group_out(n):
        lanes = pl.ds(pl.multiple_of(n * 128, 128), 128)
        return to_partner(5 + n, ql2.at[:, other, lanes], qlin.at[:, :, lanes])

    @pl.loop(0, 4)
    def _(k):
        chip = lax.rem(block + 1 + k, 4)

        @pl.loop(0, 4)
        def _(j):
            n = 2 * ((chip // 2) * 4 + (j // 2) * 2 + lax.rem(chip, 2)) + lax.rem(j, 2)
            backward(n, chip, lax.rem(j, 2) * 16 + (j // 2) * 2, f, ql2.at[0], ql2.at[1], kro, w)
            group_out(n).start()

        for c in range(2):
            to = 2 * chip + c

            @pl.when(to != part)
            def _():
                pairs_out.copy(lax.rem(to + 8 - part, 8)).start()

            @pl.when(to == part)
            def _():
                krin[part] = kro[part]

        @pl.when(k == 0)
        def _():
            mixed_out.wait()
            mixf = w["mixf"]
            for c in range(CH):
                mixf[core, c * 32:c * 32 + 32, :] = w["mx"][c, mine, :].astype(F32)
                mixf[1 - core, c * 32:c * 32 + 32, :] = w["mixin"][c].astype(F32)
            to_pairs(mixf, w["stagem"], 8, 16)
            mixed.start()
            w["recvm"][slot] = w["stagem"][slot]

    @pl.loop(0, 16)
    def _(n):
        group_out(n).wait()

    total = (ql2[:, mine, :] + qlin[...]).astype(BF16).reshape(64, 2048)
    for h in range(2):
        plain = dot(total[:, h * 1024:h * 1024 + 1024], w["pt"][...])
        for c in range(CH):
            wide[h, c * 32:c * 32 + 32, :] = plain[0:32, c * 128:c * 128 + 128]
            wide[h, 256 + c * 32:288 + c * 32, :] = plain[32:64, c * 128:c * 128 + 128]
    to_pairs(wide, w["stage3"], 16, 16, 16)
    mixed.finish()
    gu = dot(w["recvm"][...].reshape(256, 512), w["up"][...], NT).reshape(16, 16, 128)
    gws = w["gws"]
    gws[:, 32:40, :] = gu[:, 0:8]
    pairs_out.finish()
    for j in range(2):
        total = krin[j] + krin[2 + j] + krin[4 + j] + krin[6 + j]
        total = total.astype(BF16).reshape(16, 2, 16, 128)
        for a in range(2):
            w["stage3"][:, 0:16, j * 256 + a * 128:j * 256 + a * 128 + 128] = total[:, a]
    backs = over(4, HEADS, slot_peer, lambda s: w["stage3"].at[slot_at(s)], w["recv3"].at[slot])
    backs.start()
    w["recv3"][slot] = w["stage3"][slot]
    backs.finish()

    every = w["recv3"][...].reshape(512, 512)
    gws[:, 0:32, :] = dot(every, w["xp"][...], NT).reshape(16, 32, 128)
    sums = over(5, HEADS, head_peer, lambda s: gws.at[head_at(s)], w["gwin"].at[me])
    sums.start()
    w["gwin"][me] = gws[me]
    image = dot(wall[:, 0:32, :].reshape(512, 128), every, TN).reshape(16, 8, 512)
    w["stage4"][...] = jnp.concatenate([image, jnp.zeros((16, 8, 512), F32)], axis=1).astype(BF16)
    images = over(6, HEADS, head_peer, lambda s: w["stage4"].at[head_at(s)], w["recv4"].at[me])
    images.start()
    w["recv4"][me] = w["stage4"][me]
    sums.finish()
    total = w["gwin"][0]
    for p in range(1, HEADS):
        total = total + w["gwin"][p]
    w["part"][...] = total
    last = over(1, ROWS, row_peer, lambda s: w["part"], w["gwrow"].at[row])
    last.start()
    w["gwrow"][row] = total
    images.finish()
    from_pairs(w["recv4"], 0, 16, wide, 0, 32)
    for z in range(2):
        grads[:, :, z * 128:z * 128 + 128] = wide[z, 0:256, :].astype(BF16).reshape(8, 32, 128)
    last.finish()
    total = w["gwrow"][0]
    for p in range(1, ROWS):
        total = total + w["gwrow"][p]
    total = total * (1.0 / 256.0)
    for n, out in enumerate((gk, gr, gq, gl, go)):
        out[...] = total[8 * n:8 * n + 8]
    for trade in (inputs, weights, mapped, pairs_out, mixed, backs, sums, images, last):
        trade.drain()

    @pl.loop(0, 4)
    def _(g):
        near_copy(g).wait_send()

        @pl.loop(1, 8)
        def _(s):
            kr_copy(g, s).wait_send()


def layer_scratch():
    vmem, dma = pltpu.VMEM, pltpu.SemaphoreType.DMA
    return dict(
        core_scratch(),
        wide=vmem((2, 1024, 128), F32), wide2=vmem((2, 2048, 128), F32), wself=vmem((48, 128), BF16), wall=vmem((16, 48, 128), BF16),
        stage1=vmem((16, 16, 512), BF16), recv1=vmem((16, 16, 512), BF16), xp=vmem((128, 512), BF16), up=vmem((128, 512), BF16),
        stage2=vmem((16, 48, 512), BF16), recv2=vmem((16, 48, 512), BF16), near=vmem((16, 32, 512), BF16), mask=vmem((2, 32, 128), F32),
        kr=vmem((8, 16, 16, 256), BF16),
        ql2=vmem((2, 64, 2048), F32), qlin=vmem((2, 32, 2048), F32), kro=vmem((8, 32, 16, 128), F32), krin=vmem((8, 32, 16, 128), F32),
        mx=vmem((8, 64, 128), BF16), mixin=vmem((8, 32, 128), BF16), mixf=vmem((2, 256, 128), F32),
        stagem=vmem((16, 16, 512), BF16), recvm=vmem((16, 16, 512), BF16),
        stage3=vmem((16, 32, 512), BF16), recv3=vmem((16, 32, 512), BF16), stage4=vmem((16, 16, 512), BF16), recv4=vmem((16, 16, 512), BF16),
        gws=vmem((16, 40, 128), F32), gwin=vmem((16, 40, 128), F32), part=vmem((40, 128), F32), gwrow=vmem((8, 40, 128), F32),
        hs=dma((14, 16)), rs=dma((4, 8)), ps=dma((2, 21)), ks=dma((2, 4, 8)),
    )


def local(x, allowance, asking, lookup, first_content, second_content, final, scaling, upstream):
    vm = pl.BlockSpec(memory_space=pltpu.VMEM)
    names = layer_scratch()
    grads, gq, gk, gl, gr, go = pl.pallas_call(
        functools.partial(layer, list(names)),
        out_shape=[jax.ShapeDtypeStruct((8, 32, 256), BF16)] + [jax.ShapeDtypeStruct((8, 128), F32)] * 5,
        in_specs=[vm] * 8 + [pl.BlockSpec(memory_space=pltpu.SMEM)], out_specs=[vm] * 6,
        scratch_shapes=list(names.values()),
        compiler_params=pltpu.CompilerParams(collective_id=0, has_side_effects=True, vmem_limit_bytes=56 * 2 ** 20),
        name="layer",
    )(x, upstream, asking.T, lookup.T, first_content.T, second_content.T, final, allowance, scaling)
    return grads, gq.T, gk.T, gl.T, gr.T, go


def solution(mesh):
    pairs, columns = P("head", "row", None), P(None, "head")
    placed = (pairs, P("row", None), columns, columns, columns, columns, P("head", None), P("head"), pairs)
    return jax.shard_map(
        local, mesh=mesh, in_specs=placed,
        out_specs=(pairs, columns, columns, columns, columns, P("head", None)), check_vma=False,
    )
```

time: 160 us -> 136 us (0.85)
  Pallas kernels: 153 us -> 129 us
    pallas_call x1, Pallas kernels: 153 us -> 129 us  [local(): pl.pallas_call(functools.partial(layer, list(names)), out_shape=[jax.Shap...]
where the time goes in v3:
time: 136 us; the launch traced here: 135 us
  Pallas kernels  129 us (95%)
  local copies, waits for them, and re-layouts  4.88 us (4%)
    pallas_call x1, Pallas kernels, local(): pl.pallas_call(functools.partial(layer, list(names)), out_shape=[jax.Shap...  129 us
    unnamed x16, local copies, waits for them, and re-layouts  4.88 us

profile of v3, /device:TPU:1, one launch (start us, length us, event | category | flops | bytes accessed | tf_op | source)
XLA Modules:
  0.0 135.3 jit_solution(9697403483686323254)
XLA Ops:
  1.3 129.1 %layer.1 = (bf16[8,32,256]{2,1,0:T(8,128)(2,1)}, f32[8,128]{1,0:T(8,128)}, f32[8,128]{1,0:T(8,128)}, f32[8,128]{1,0:T(8,128)}, f32[8,128]{1,0:T(8,128)}, /*index=5*/f32[8,128]{1,0:T(8,128)}) custom-call(bf16[8,32,256]{2,1,0:T(8,128)(2,1)} %x.1, bf16[8,32,256]{2,1,0:T(8,128)(2,1)} %u.1, bf16[8,128]{1,0:T(8,128)(2,1)} %bitcast.12, bf16[8,128]{1,0:T(8,128)(2,1)} %bitcast.13, ...), custom_call_target="tpu_custom_call" | custom-call | tf_op jit(solution)/shard_map/layer/pallas_call | solution.py:523
  130.4 0.0 copy-start.4
  130.4 1.6 %copy.22 = bf16[8,32,256]{2,1,0:T(8,128)(2,1)} copy(bf16[8,32,256]{2,1,0:T(8,128)(2,1)} %get-tuple-element.24) | data formatting | bytes 262144
  131.9 0.0 copy-done.4
  131.9 0.0 copy-start.3
  131.9 0.6 copy.23
  132.5 0.1 copy-done.3
  132.6 0.0 copy-start.2
  132.6 0.6 copy.24
  133.2 0.1 copy-done.2
  133.3 0.0 copy-start.1
  133.3 0.6 copy.25
  133.9 0.1 copy-done.1
  134.0 0.0 copy-start
  134.0 0.6 copy.26
  134.6 0.1 copy-done
  134.7 0.6 copy.27
Async XLA Ops:
  130.4 1.6 %copy-start.4 = (f32[8,128]{1,0:T(8,128)S(1)}, f32[8,128]{1,0:T(8,128)}, u32[]{:S(2)}) copy-start(f32[8,128]{1,0:T(8,128)} %get-tuple-element.13) | copy-start | bytes 12292
  131.9 0.7 copy-start.3
  132.6 0.7 copy-start.2
  133.3 0.7 copy-start.1
  134.0 0.7 copy-start

commit v4 on v3

--- a/solution.py
+++ b/solution.py
@@ -82,9 +82,9 @@
 
 
 def forward(wide, mine, f, mixed, w):
-    @pl.loop(0, 4)
+    @pl.loop(0, 2)
     def _(ip):
-        rows = pl.ds(pl.multiple_of(ip * 16, 16), 16)
+        rows = pl.ds(pl.multiple_of(ip * 32, 32), 32)
         top = w["m"][rows, :]
 
         def step(n, carry):
@@ -92,24 +92,23 @@
             acc = list(acc)
             tile = w["lb16"][rows, pl.ds(pl.multiple_of(n * 128, 128), 128)]
             lhs = jnp.concatenate([tile * w["mt"][t:t + 1, :128] for t in range(16)], axis=0)
-            spread = dot(lhs, w["wc"][...])
+            rg = w["rf"][pl.ds(pl.multiple_of(n * 128, 128), 128), :].astype(BF16)
+            both = dot(lhs, jnp.concatenate([rg] * CH, axis=1) * w["wc"][...])
             for t in range(16):
                 lv = n * 16 + t
                 wt = jnp.exp(f * (w["s"][lv, rows, :] - top))
                 w["s"][lv, rows, :] = wt
                 total = total + wt
-                rr = w["rf"][pl.ds(pl.multiple_of(lv * 8, 8), 8), :]
                 for c in range(CH):
-                    lb = spread[t * 16:t * 16 + 16, c * 128:c * 128 + 128]
-                    acc[c] = acc[c] + (wt * rr[c:c + 1, :]) * lb
+                    acc[c] = acc[c] + wt * both[t * 32:t * 32 + 32, c * 128:c * 128 + 128]
             return total, tuple(acc)
 
-        zero = jnp.zeros((16, J), F32)
-        total, acc = lax.fori_loop(0, 16, step, (zero, (zero,) * CH))
+        zero = jnp.zeros((32, J), F32)
+        total, acc = lax.fori_loop(0, 16, step, (zero, (zero,) * CH), unroll=4)
         inv = 1.0 / total
         delta = zero
         for c in range(CH):
-            gc = wide[mine, pl.ds(pl.multiple_of((16 + c) * I + ip * 16, 16), 16), :]
+            gc = wide[mine, pl.ds(pl.multiple_of((16 + c) * I + ip * 32, 32), 32), :]
             mc = acc[c] * inv
             mixed[c, rows, :] = mc.astype(BF16)
             delta = delta + gc * mc
@@ -131,10 +130,11 @@
         rb = [jnp.broadcast_to(rr[c:c + 1, :], (8, J)) for c in range(CH)]
         br = [jnp.zeros((8, J), F32) for c in range(CH)]
         base = t * 8
-        halves = [[] for c in range(CH)]
+        lanes8 = lax.broadcasted_iota(jnp.int32, (8, 128), 1)
         for it in range(8):
             rows = slice(it * 8, it * 8 + 8)
             wt = w["s"][lv, rows, :]
+            blt = bl2[rows, at]
             pgp = None
             for c in range(CH):
                 x = wt * w["gs"][c, rows, :]
@@ -142,13 +142,10 @@
                 br[c] = br[c] + xl
                 term = xl * rb[c]
                 pgp = term if pgp is None else pgp + term
-                halves[c].append(x)
+                red = jnp.sum(x * rb[c], axis=1, keepdims=True)
+                blt = jnp.where(lanes8 == base + c, red, blt)
             w["e"][t, rows, :] = pgp - wt * w["ds"][rows, :]
-        blt = bl2[:, at]
-        for c in range(CH):
-            red = jnp.sum(jnp.concatenate(halves[c], axis=0) * rr[c:c + 1, :], axis=1, keepdims=True)
-            blt = jnp.where(lanes64 == base + c, red, blt)
-        bl2[:, at] = blt
+            bl2[rows, at] = blt
         slot = lax.rem(t, 2)
         for c in range(CH):
             w["br8"][slot, c * 8:c * 8 + 8, :] = br[c]
@@ -228,14 +225,15 @@
             stage[i // 2, first:first + rows, at:at + 128] = piece.astype(BF16)
 
 
-def from_pairs(recv, lo, hi, wide, offset, stride):
-    for i in range(32):
+def from_pairs(recv, lo, hi, wide, offset, stride, first=0, count=16):
+    for i in range(2 * count):
         for z in range(2):
             at = lane_of(i, z)
-            wide[z, pl.ds(offset + i, hi - lo, stride=stride), :] = recv[i // 2, lo:hi, at:at + 128].astype(F32)
-
-
-def layer(names, x, u, wq, wk, wl, wr, wf, allowance, fac, grads, gq, gk, gl, gr, go, *scratch):
+            rows = pl.ds(offset + first * 2 + i, hi - lo, stride=stride)
+            wide[z, rows, :] = recv[first + i // 2, lo:hi, at:at + 128].astype(F32)
+
+
+def layer(names, x, u, wq, wk, wl, wr, wf, allowance, fac, grads, gw, *scratch):
     w = dict(zip(names, scratch))
     me, row = lax.axis_index("head"), lax.axis_index("row")
     core = lax.rem(me, 2)
@@ -322,16 +320,25 @@
             else:
                 recv2[slot] = stage2[slot]
 
+    near, wide2 = w["near"], w["wide2"]
+
+    def four(g):
+        return lax.rem(slot // 4 + 4 - g, 4) * 4
+
     def kr_copy(g, s):
-        four = pl.ds(lax.rem(slot // 4 + 4 - g, 4) * 4, 4)
+        some = pl.ds(four(g), 4)
         to = lax.rem(part + s, 8)
         return pltpu.make_async_remote_copy(
-            src_ref=recv2.at[four, pl.ds(0, 16), pl.ds(pl.multiple_of(lax.rem(to, 2) * 256, 128), 256)], dst_ref=kr.at[part, four],
+            src_ref=recv2.at[some, pl.ds(0, 16), pl.ds(pl.multiple_of(lax.rem(to, 2) * 256, 128), 256)], dst_ref=kr.at[part, some],
             send_sem=w["ks"].at[0, g, s], recv_sem=w["ks"].at[1, g, s], device_id=part_peer(s), device_id_type=MESH)
 
     def near_copy(g):
-        four = pl.ds(lax.rem(slot // 4 + 4 - g, 4) * 4, 4)
-        return to_partner(g, recv2.at[four, pl.ds(16, 32)], w["near"].at[four])
+        some = pl.ds(four(g), 4)
+        return to_partner(g, recv2.at[some, pl.ds(16, 32)], near.at[some])
+
+    def unpack_near(g):
+        near_copy(g).wait_recv()
+        from_pairs(near, 0, 32, wide2, 32 - core * 32, I, four(g), 4)
 
     @pl.loop(0, 4)
     def _(g):
@@ -347,16 +354,14 @@
         def _(s):
             kr_copy(g, s).start()
 
-    near = w["near"]
-    wide2 = w["wide2"]
+        from_pairs(recv2, 16, 48, wide2, core * 32, I, four(g), 4)
+
+        @pl.when(g > 0)
+        def _():
+            unpack_near(g - 1)
+
+    unpack_near(3)
     own = pl.multiple_of(core * 32, 32)
-    from_pairs(recv2, 16, 48, wide2, core * 32, I)
-
-    @pl.loop(0, 4)
-    def _(g):
-        near_copy(g).wait_recv()
-
-    from_pairs(near, 0, 32, wide2, 32 - core * 32, I)
     prepare(wide2, w)
 
     f = jnp.sum(wall[slot, 32:48].astype(F32)[8:16], axis=0, keepdims=True)
@@ -443,28 +448,34 @@
         for c in range(CH):
             wide[h, c * 32:c * 32 + 32, :] = plain[0:32, c * 128:c * 128 + 128]
             wide[h, 256 + c * 32:288 + c * 32, :] = plain[32:64, c * 128:c * 128 + 128]
-    to_pairs(wide, w["stage3"], 16, 16, 16)
+    stage3, recv3 = w["stage3"], w["recv3"]
+    to_pairs(wide, stage3.at[1], 16, 16)
+    backs = [over(4 + 3 * n, HEADS, slot_peer, lambda s, n=n: stage3.at[n, slot_at(s)], recv3.at[n, slot]) for n in range(2)]
+    backs[1].start()
+    recv3[1, slot] = stage3[1, slot]
     mixed.finish()
-    gu = dot(w["recvm"][...].reshape(256, 512), w["up"][...], NT).reshape(16, 16, 128)
     gws = w["gws"]
-    gws[:, 32:40, :] = gu[:, 0:8]
+    gws[:, 32:40, :] = dot(w["recvm"][...].reshape(256, 512), w["up"][...], NT).reshape(16, 16, 128)[:, 0:8]
     pairs_out.finish()
     for j in range(2):
         total = krin[j] + krin[2 + j] + krin[4 + j] + krin[6 + j]
         total = total.astype(BF16).reshape(16, 2, 16, 128)
         for a in range(2):
-            w["stage3"][:, 0:16, j * 256 + a * 128:j * 256 + a * 128 + 128] = total[:, a]
-    backs = over(4, HEADS, slot_peer, lambda s: w["stage3"].at[slot_at(s)], w["recv3"].at[slot])
-    backs.start()
-    w["recv3"][slot] = w["stage3"][slot]
-    backs.finish()
-
-    every = w["recv3"][...].reshape(512, 512)
-    gws[:, 0:32, :] = dot(every, w["xp"][...], NT).reshape(16, 32, 128)
+            stage3[0, :, :, j * 256 + a * 128:j * 256 + a * 128 + 128] = total[:, a]
+    backs[0].start()
+    recv3[0, slot] = stage3[0, slot]
+
+    image = None
+    for n in (1, 0):
+        backs[n].finish()
+        every = recv3[n].reshape(256, 512)
+        gws[:, 16 * n:16 * n + 16, :] = dot(every, w["xp"][...], NT).reshape(16, 16, 128)
+        term = dot(wall[:, 16 * n:16 * n + 16, :].reshape(256, 128), every, TN)
+        image = term if image is None else image + term
     sums = over(5, HEADS, head_peer, lambda s: gws.at[head_at(s)], w["gwin"].at[me])
     sums.start()
     w["gwin"][me] = gws[me]
-    image = dot(wall[:, 0:32, :].reshape(512, 128), every, TN).reshape(16, 8, 512)
+    image = image.reshape(16, 8, 512)
     w["stage4"][...] = jnp.concatenate([image, jnp.zeros((16, 8, 512), F32)], axis=1).astype(BF16)
     images = over(6, HEADS, head_peer, lambda s: w["stage4"].at[head_at(s)], w["recv4"].at[me])
     images.start()
@@ -485,10 +496,8 @@
     total = w["gwrow"][0]
     for p in range(1, ROWS):
         total = total + w["gwrow"][p]
-    total = total * (1.0 / 256.0)
-    for n, out in enumerate((gk, gr, gq, gl, go)):
-        out[...] = total[8 * n:8 * n + 8]
-    for trade in (inputs, weights, mapped, pairs_out, mixed, backs, sums, images, last):
+    gw[...] = total * (1.0 / 256.0)
+    for trade in (inputs, weights, mapped, pairs_out, mixed, *backs, sums, images, last):
         trade.drain()
 
     @pl.loop(0, 4)
@@ -498,6 +507,12 @@
         @pl.loop(1, 8)
         def _(s):
             kr_copy(g, s).wait_send()
+
+
+def results(grads, gw, out, gq, gk, gl, gr, go):
+    out[...] = grads[...]
+    for n, ref in enumerate((gk, gr, gq, gl, go)):
+        ref[...] = gw[8 * n:8 * n + 8, :]
 
 
 def layer_scratch():
@@ -511,23 +526,27 @@
         ql2=vmem((2, 64, 2048), F32), qlin=vmem((2, 32, 2048), F32), kro=vmem((8, 32, 16, 128), F32), krin=vmem((8, 32, 16, 128), F32),
         mx=vmem((8, 64, 128), BF16), mixin=vmem((8, 32, 128), BF16), mixf=vmem((2, 256, 128), F32),
         stagem=vmem((16, 16, 512), BF16), recvm=vmem((16, 16, 512), BF16),
-        stage3=vmem((16, 32, 512), BF16), recv3=vmem((16, 32, 512), BF16), stage4=vmem((16, 16, 512), BF16), recv4=vmem((16, 16, 512), BF16),
+        stage3=vmem((2, 16, 16, 512), BF16), recv3=vmem((2, 16, 16, 512), BF16), stage4=vmem((16, 16, 512), BF16), recv4=vmem((16, 16, 512), BF16),
         gws=vmem((16, 40, 128), F32), gwin=vmem((16, 40, 128), F32), part=vmem((40, 128), F32), gwrow=vmem((8, 40, 128), F32),
-        hs=dma((14, 16)), rs=dma((4, 8)), ps=dma((2, 21)), ks=dma((2, 4, 8)),
+        hs=dma((16, 16)), rs=dma((4, 8)), ps=dma((2, 21)), ks=dma((2, 4, 8)),
     )
 
 
 def local(x, allowance, asking, lookup, first_content, second_content, final, scaling, upstream):
     vm = pl.BlockSpec(memory_space=pltpu.VMEM)
     names = layer_scratch()
-    grads, gq, gk, gl, gr, go = pl.pallas_call(
+    grads, gw = pl.pallas_call(
         functools.partial(layer, list(names)),
-        out_shape=[jax.ShapeDtypeStruct((8, 32, 256), BF16)] + [jax.ShapeDtypeStruct((8, 128), F32)] * 5,
-        in_specs=[vm] * 8 + [pl.BlockSpec(memory_space=pltpu.SMEM)], out_specs=[vm] * 6,
+        out_shape=[jax.ShapeDtypeStruct((8, 32, 256), BF16), jax.ShapeDtypeStruct((40, 128), F32)],
+        in_specs=[vm] * 8 + [pl.BlockSpec(memory_space=pltpu.SMEM)], out_specs=[vm] * 2,
         scratch_shapes=list(names.values()),
         compiler_params=pltpu.CompilerParams(collective_id=0, has_side_effects=True, vmem_limit_bytes=56 * 2 ** 20),
         name="layer",
     )(x, upstream, asking.T, lookup.T, first_content.T, second_content.T, final, allowance, scaling)
+    grads, gq, gk, gl, gr, go = pl.pallas_call(
+        results, out_shape=[jax.ShapeDtypeStruct((8, 32, 256), BF16)] + [jax.ShapeDtypeStruct((8, 128), F32)] * 5,
+        in_specs=[vm] * 2, out_specs=[vm] * 6, name="results",
+    )(grads, gw)
     return grads, gq.T, gk.T, gl.T, gr.T, go
 
 

time: 136 us -> 124 us (0.912)
  Pallas kernels: 129 us -> 122 us
  local copies, waits for them, and re-layouts: 4.88 us -> 0 us
    pallas_call x1, Pallas kernels: 129 us -> 121 us  [local(): pl.pallas_call(functools.partial(layer, list(names)), out_shape=[jax.Shap...]
    unnamed x16 -> x0, local copies, waits for them, and re-layouts: 4.88 us -> none
    pallas_call x0 -> x1, Pallas kernels: none -> 1.58 us  [local(): pl.pallas_call(results, out_shape=[jax.ShapeDtypeStruct((8, 32, 256), BF1...]
where the time goes in v4:
time: 124 us
  Pallas kernels  122 us (98%)
  between operations  1.29 us (1%)
    pallas_call x1, Pallas kernels, local(): pl.pallas_call(functools.partial(layer, list(names)), out_shape=[jax.Shap...  121 us

profile of v4, /device:TPU:1, one launch (start us, length us, event | category | flops | bytes accessed | tf_op | source)
XLA Modules:
  0.0 123.6 jit_solution(15845560137769503575)
XLA Ops:
  1.3 120.7 %layer.1 = (bf16[8,32,256]{2,1,0:T(8,128)(2,1)}, f32[40,128]{1,0:T(8,128)}) custom-call(bf16[8,32,256]{2,1,0:T(8,128)(2,1)} %x.1, bf16[8,32,256]{2,1,0:T(8,128)(2,1)} %u.1, bf16[8,128]{1,0:T(8,128)(2,1)} %bitcast.8, bf16[8,128]{1,0:T(8,128)(2,1)} %bitcast.9, bf16[8,128]{1,0:T(8,128)(2,1)} %bitcast.10, bf16[8,128]{1,0:T(8,128)(2,1)} %bitcast.11, ...), custom_call_target="tpu_custom_call" | custom-call | tf_op jit(solution)/shard_map/layer/pallas_call | solution.py:538
  122.0 1.6 %results.1 = (bf16[8,32,256]{2,1,0:T(8,128)(2,1)}, f32[8,128]{1,0:T(8,128)}, f32[8,128]{1,0:T(8,128)}, f32[8,128]{1,0:T(8,128)}, f32[8,128]{1,0:T(8,128)}, /*index=5*/f32[8,128]{1,0:T(8,128)}) custom-call(bf16[8,32,256]{2,1,0:T(8,128)(2,1)} %get-tuple-element.14.grads, f32[40,128]{1,0:T(8,128)} %get-tuple-element.15.gw), custom_call_target="tpu_custom_call" | custom-call | tf_op jit(solution)/shard_map/results/pallas_call | solution.py:546

commit v5 on v4

--- a/solution.py
+++ b/solution.py
@@ -28,7 +28,7 @@
         k2=pltpu.VMEM((2048, J), BF16), mt=pltpu.VMEM((16, 256), BF16), wc=pltpu.VMEM((128, 1024), BF16), lb16=pltpu.VMEM((I, 2048), BF16),
         s=pltpu.VMEM((L, I, J), F32), m=pltpu.VMEM((I, J), F32), gs=pltpu.VMEM((CH, I, J), F32), ds=pltpu.VMEM((I, J), F32),
 
-        e=pltpu.VMEM((16, I, J), F32), br8=pltpu.VMEM((2, 64, J), F32),
+        e=pltpu.VMEM((16, I, J), F32), br8=pltpu.VMEM((16, 64, J), F32),
     )
 
 
@@ -127,12 +127,12 @@
         pick = jnp.where((lanes64 >> 3) == t, 1.0, 0.0).astype(BF16)
         spread = dot(w["lb16"][:, at] * pick, w["wc"][...])
         rr = w["rf"][pl.ds(pl.multiple_of(lv * 8, 8), 8), :]
-        rb = [jnp.broadcast_to(rr[c:c + 1, :], (8, J)) for c in range(CH)]
-        br = [jnp.zeros((8, J), F32) for c in range(CH)]
+        rb = [jnp.broadcast_to(rr[c:c + 1, :], (16, J)) for c in range(CH)]
+        br = [jnp.zeros((16, J), F32) for c in range(CH)]
         base = t * 8
-        lanes8 = lax.broadcasted_iota(jnp.int32, (8, 128), 1)
-        for it in range(8):
-            rows = slice(it * 8, it * 8 + 8)
+        lanes16 = lax.broadcasted_iota(jnp.int32, (16, 128), 1)
+        for it in range(4):
+            rows = slice(it * 16, it * 16 + 16)
             wt = w["s"][lv, rows, :]
             blt = bl2[rows, at]
             pgp = None
@@ -143,17 +143,17 @@
                 term = xl * rb[c]
                 pgp = term if pgp is None else pgp + term
                 red = jnp.sum(x * rb[c], axis=1, keepdims=True)
-                blt = jnp.where(lanes8 == base + c, red, blt)
+                blt = jnp.where(lanes16 == base + c, red, blt)
             w["e"][t, rows, :] = pgp - wt * w["ds"][rows, :]
             bl2[rows, at] = blt
-        slot = lax.rem(t, 2)
         for c in range(CH):
-            w["br8"][slot, c * 8:c * 8 + 8, :] = br[c]
-        tot = w["br8"][slot, pl.ds(0, 8, stride=8), :]
+            w["br8"][t, c * 8:c * 8 + 8, :] = br[c][:8] + br[c][8:]
+
+    for t in range(16):
+        tot = w["br8"][t, pl.ds(0, 8, stride=8), :]
         for z in range(1, 8):
-            tot = tot + w["br8"][slot, pl.ds(z, 8, stride=8), :]
-        kro[2 * chip + lax.rem(t // 2, 2), place + (t // 4) * 4 + lax.rem(t, 2), 8:16, :] = tot
-
+            tot = tot + w["br8"][t, pl.ds(z, 8, stride=8), :]
+        kro[2 * chip + (t // 2) % 2, place + (t // 4) * 4 + t % 2, 8:16, :] = tot
     ev = w["e"][...].reshape(16 * I, J)
     hi = ev.astype(BF16)
     lo = (ev - hi.astype(F32)).astype(BF16)
@@ -399,33 +399,67 @@
     mixed_out = to_partner(4, w["mx"].at[:, other], w["mixin"])
     mixed_out.start()
     ql2, qlin, kro, krin = w["ql2"], w["qlin"], w["kro"], w["krin"]
-    pairs_out = over(0, 8, part_peer, lambda s: kro.at[lax.rem(part + s, 8)], krin.at[part])
+    stageq, recvq = w["stageq"], w["recvq"]
+
+    def out_copy(y, to):
+        s = lax.rem(to + 8 - part, 8)
+        rows = pl.ds(y * 16, 16)
+        return pltpu.make_async_remote_copy(
+            src_ref=kro.at[to, rows], dst_ref=krin.at[part, rows], send_sem=w["os"].at[y, 0, s], recv_sem=w["os"].at[y, 1, s],
+            device_id=part_peer(s), device_id_type=MESH)
+
     mixed = over(3, HEADS, slot_peer, lambda s: w["stagem"].at[slot_at(s)], w["recvm"].at[slot])
 
     def group_out(n):
         lanes = pl.ds(pl.multiple_of(n * 128, 128), 128)
         return to_partner(5 + n, ql2.at[:, other, lanes], qlin.at[:, :, lanes])
 
+    def half_out(h, n):
+        @pl.loop(0, 8)
+        def _(g):
+            group_out(8 * h + g).wait()
+
+        lanes = pl.ds(pl.multiple_of(h * 1024, 1024), 1024)
+        total = (ql2[:, mine, lanes] + qlin[:, :, lanes]).astype(BF16).reshape(64, 1024)
+        plain = dot(total, w["pt"][...])
+        for c in range(CH):
+            wide[n, c * 32:c * 32 + 32, :] = plain[0:32, c * 128:c * 128 + 128]
+            wide[n, 256 + c * 32:288 + c * 32, :] = plain[32:64, c * 128:c * 128 + 128]
+        for i in range(32):
+            stageq[n, i // 2, :, (i % 2) * 128:(i % 2) * 128 + 128] = wide[n, pl.ds(i, 16, stride=32), :].astype(BF16)
+        halves[n].start()
+        recvq[h, slot] = stageq[n, slot]
+
+    far = 1 - y_lo
+    halves = [over(4 + 3 * n, HEADS, slot_peer, lambda s, n=n: stageq.at[n, slot_at(s)], recvq.at[h, slot]) for n, h in enumerate((far, y_lo))]
+
     @pl.loop(0, 4)
     def _(k):
-        chip = lax.rem(block + 1 + k, 4)
+        cy, cx = lax.rem(y_lo + 1 + k // 2, 2), lax.rem(x_lo + (k + 1) // 2, 2)
+        chip = cy * 2 + cx
 
         @pl.loop(0, 4)
         def _(j):
-            n = 2 * ((chip // 2) * 4 + (j // 2) * 2 + lax.rem(chip, 2)) + lax.rem(j, 2)
-            backward(n, chip, lax.rem(j, 2) * 16 + (j // 2) * 2, f, ql2.at[0], ql2.at[1], kro, w)
+            n = 2 * (cy * 4 + lax.rem(j, 2) * 2 + cx) + j // 2
+            backward(n, chip, (j // 2) * 16 + lax.rem(j, 2) * 2, f, ql2.at[0], ql2.at[1], kro, w)
             group_out(n).start()
 
-        for c in range(2):
-            to = 2 * chip + c
-
-            @pl.when(to != part)
+            @pl.when(lax.rem(j, 2) == 1)
             def _():
-                pairs_out.copy(lax.rem(to + 8 - part, 8)).start()
-
-            @pl.when(to == part)
-            def _():
-                krin[part] = kro[part]
+                for c in range(2):
+                    to = 2 * chip + c
+
+                    @pl.when(to != part)
+                    def _():
+                        out_copy(j // 2, to).start()
+
+        @pl.when(k == 3)
+        def _():
+            krin[part] = kro[part]
+
+        @pl.when(k == 2)
+        def _():
+            half_out(far, 0)
 
         @pl.when(k == 0)
         def _():
@@ -438,37 +472,35 @@
             mixed.start()
             w["recvm"][slot] = w["stagem"][slot]
 
-    @pl.loop(0, 16)
-    def _(n):
-        group_out(n).wait()
-
-    total = (ql2[:, mine, :] + qlin[...]).astype(BF16).reshape(64, 2048)
-    for h in range(2):
-        plain = dot(total[:, h * 1024:h * 1024 + 1024], w["pt"][...])
-        for c in range(CH):
-            wide[h, c * 32:c * 32 + 32, :] = plain[0:32, c * 128:c * 128 + 128]
-            wide[h, 256 + c * 32:288 + c * 32, :] = plain[32:64, c * 128:c * 128 + 128]
-    stage3, recv3 = w["stage3"], w["recv3"]
-    to_pairs(wide, stage3.at[1], 16, 16)
-    backs = [over(4 + 3 * n, HEADS, slot_peer, lambda s, n=n: stage3.at[n, slot_at(s)], recv3.at[n, slot]) for n in range(2)]
-    backs[1].start()
-    recv3[1, slot] = stage3[1, slot]
+    half_out(y_lo, 1)
     mixed.finish()
     gws = w["gws"]
     gws[:, 32:40, :] = dot(w["recvm"][...].reshape(256, 512), w["up"][...], NT).reshape(16, 16, 128)[:, 0:8]
-    pairs_out.finish()
+
+    @pl.loop(1, 8)
+    def _(s):
+        for y in range(2):
+            out_copy(y, lax.rem(part + s, 8)).wait_recv()
+
+    stage3, recv3 = w["stage3"], w["recv3"]
     for j in range(2):
         total = krin[j] + krin[2 + j] + krin[4 + j] + krin[6 + j]
         total = total.astype(BF16).reshape(16, 2, 16, 128)
         for a in range(2):
-            stage3[0, :, :, j * 256 + a * 128:j * 256 + a * 128 + 128] = total[:, a]
-    backs[0].start()
-    recv3[0, slot] = stage3[0, slot]
+            stage3[:, :, j * 256 + a * 128:j * 256 + a * 128 + 128] = total[:, a]
+    backs = over(8, HEADS, slot_peer, lambda s: stage3.at[slot_at(s)], recv3.at[slot])
+    backs.start()
+    recv3[slot] = stage3[slot]
 
     image = None
     for n in (1, 0):
-        backs[n].finish()
-        every = recv3[n].reshape(256, 512)
+        if n:
+            halves[0].finish()
+            halves[1].finish()
+            every = jnp.concatenate([recvq[0].reshape(256, 256), recvq[1].reshape(256, 256)], axis=1)
+        else:
+            backs.finish()
+            every = recv3[...].reshape(256, 512)
         gws[:, 16 * n:16 * n + 16, :] = dot(every, w["xp"][...], NT).reshape(16, 16, 128)
         term = dot(wall[:, 16 * n:16 * n + 16, :].reshape(256, 128), every, TN)
         image = term if image is None else image + term
@@ -476,7 +508,7 @@
     sums.start()
     w["gwin"][me] = gws[me]
     image = image.reshape(16, 8, 512)
-    w["stage4"][...] = jnp.concatenate([image, jnp.zeros((16, 8, 512), F32)], axis=1).astype(BF16)
+    w["stage4"][...] = jnp.concatenate([image[:, :, 0:256], image[:, :, 256:512]], axis=1).astype(BF16)
     images = over(6, HEADS, head_peer, lambda s: w["stage4"].at[head_at(s)], w["recv4"].at[me])
     images.start()
     w["recv4"][me] = w["stage4"][me]
@@ -489,7 +521,10 @@
     last.start()
     w["gwrow"][row] = total
     images.finish()
-    from_pairs(w["recv4"], 0, 16, wide, 0, 32)
+    for i in range(32):
+        two = w["recv4"][i // 2, :, (i % 2) * 128:(i % 2) * 128 + 128].astype(F32)
+        for z in range(2):
+            wide[z, pl.ds(i, 8, stride=32), :] = two[z * 8:z * 8 + 8]
     for z in range(2):
         grads[:, :, z * 128:z * 128 + 128] = wide[z, 0:256, :].astype(BF16).reshape(8, 32, 128)
     last.finish()
@@ -497,7 +532,7 @@
     for p in range(1, ROWS):
         total = total + w["gwrow"][p]
     gw[...] = total * (1.0 / 256.0)
-    for trade in (inputs, weights, mapped, pairs_out, mixed, *backs, sums, images, last):
+    for trade in (inputs, weights, mapped, mixed, *halves, backs, sums, images, last):
         trade.drain()
 
     @pl.loop(0, 4)
@@ -507,6 +542,11 @@
         @pl.loop(1, 8)
         def _(s):
             kr_copy(g, s).wait_send()
+
+    @pl.loop(1, 8)
+    def _(s):
+        for y in range(2):
+            out_copy(y, lax.rem(part + s, 8)).wait_send()
 
 
 def results(grads, gw, out, gq, gk, gl, gr, go):
@@ -526,9 +566,9 @@
         ql2=vmem((2, 64, 2048), F32), qlin=vmem((2, 32, 2048), F32), kro=vmem((8, 32, 16, 128), F32), krin=vmem((8, 32, 16, 128), F32),
         mx=vmem((8, 64, 128), BF16), mixin=vmem((8, 32, 128), BF16), mixf=vmem((2, 256, 128), F32),
         stagem=vmem((16, 16, 512), BF16), recvm=vmem((16, 16, 512), BF16),
-        stage3=vmem((2, 16, 16, 512), BF16), recv3=vmem((2, 16, 16, 512), BF16), stage4=vmem((16, 16, 512), BF16), recv4=vmem((16, 16, 512), BF16),
+        stage3=vmem((16, 16, 512), BF16), recv3=vmem((16, 16, 512), BF16), stageq=vmem((2, 16, 16, 256), BF16), recvq=vmem((2, 16, 16, 256), BF16), stage4=vmem((16, 16, 256), BF16), recv4=vmem((16, 16, 256), BF16),
         gws=vmem((16, 40, 128), F32), gwin=vmem((16, 40, 128), F32), part=vmem((40, 128), F32), gwrow=vmem((8, 40, 128), F32),
-        hs=dma((16, 16)), rs=dma((4, 8)), ps=dma((2, 21)), ks=dma((2, 4, 8)),
+        os=dma((2, 2, 8)), hs=dma((18, 16)), rs=dma((4, 8)), ps=dma((2, 21)), ks=dma((2, 4, 8)),
     )
 
 

time: 124 us -> 120 us (0.968)
  Pallas kernels: 122 us -> 119 us
    pallas_call x1, Pallas kernels: 121 us -> 117 us  [local(): pl.pallas_call(functools.partial(layer, list(names)), out_shape=[jax.Shap...]
where the time goes in v5:
time: 120 us
  Pallas kernels  119 us (99%)
  between operations  1.29 us (1%)
    pallas_call x1, Pallas kernels, local(): pl.pallas_call(functools.partial(layer, list(names)), out_shape=[jax.Shap...  117 us

profile of v5, /device:TPU:1, one launch (start us, length us, event | category | flops | bytes accessed | tf_op | source)
XLA Modules:
  0.0 120.2 jit_solution(7830627094791160296)
XLA Ops:
  1.3 117.3 %layer.1 = (bf16[8,32,256]{2,1,0:T(8,128)(2,1)}, f32[40,128]{1,0:T(8,128)}) custom-call(bf16[8,32,256]{2,1,0:T(8,128)(2,1)} %x.1, bf16[8,32,256]{2,1,0:T(8,128)(2,1)} %u.1, bf16[8,128]{1,0:T(8,128)(2,1)} %bitcast.8, bf16[8,128]{1,0:T(8,128)(2,1)} %bitcast.9, bf16[8,128]{1,0:T(8,128)(2,1)} %bitcast.10, bf16[8,128]{1,0:T(8,128)(2,1)} %bitcast.11, ...), custom_call_target="tpu_custom_call" | custom-call | tf_op jit(solution)/shard_map/layer/pallas_call | solution.py:578
  118.6 1.6 %results.1 = (bf16[8,32,256]{2,1,0:T(8,128)(2,1)}, f32[8,128]{1,0:T(8,128)}, f32[8,128]{1,0:T(8,128)}, f32[8,128]{1,0:T(8,128)}, f32[8,128]{1,0:T(8,128)}, /*index=5*/f32[8,128]{1,0:T(8,128)}) custom-call(bf16[8,32,256]{2,1,0:T(8,128)(2,1)} %get-tuple-element.14.grads, f32[40,128]{1,0:T(8,128)} %get-tuple-element.15.gw), custom_call_target="tpu_custom_call" | custom-call | tf_op jit(solution)/shard_map/results/pallas_call | solution.py:586

commit v6 on v5

--- a/solution.py
+++ b/solution.py
@@ -433,35 +433,37 @@
     far = 1 - y_lo
     halves = [over(4 + 3 * n, HEADS, slot_peer, lambda s, n=n: stageq.at[n, slot_at(s)], recvq.at[h, slot]) for n, h in enumerate((far, y_lo))]
 
-    @pl.loop(0, 4)
+    @pl.loop(0, 8)
     def _(k):
-        cy, cx = lax.rem(y_lo + 1 + k // 2, 2), lax.rem(x_lo + (k + 1) // 2, 2)
+        first, last_two, odd = 1 - (k + 6) // 8, k // 6, lax.rem(k, 2)
+        between = 1 - first - last_two
+        cy = lax.rem(y_lo + first + between * (1 - odd), 2)
+        cx = lax.rem(x_lo + first + between * odd, 2)
+        yh = (first + last_two) * odd + between * (k // 2 - 1)
         chip = cy * 2 + cx
 
-        @pl.loop(0, 4)
+        @pl.loop(0, 2)
         def _(j):
-            n = 2 * (cy * 4 + lax.rem(j, 2) * 2 + cx) + j // 2
-            backward(n, chip, (j // 2) * 16 + lax.rem(j, 2) * 2, f, ql2.at[0], ql2.at[1], kro, w)
+            n = 2 * (cy * 4 + j * 2 + cx) + yh
+            backward(n, chip, yh * 16 + j * 2, f, ql2.at[0], ql2.at[1], kro, w)
             group_out(n).start()
 
-            @pl.when(lax.rem(j, 2) == 1)
+        for c in range(2):
+            to = 2 * chip + c
+
+            @pl.when(to != part)
             def _():
-                for c in range(2):
-                    to = 2 * chip + c
-
-                    @pl.when(to != part)
-                    def _():
-                        out_copy(j // 2, to).start()
-
-        @pl.when(k == 3)
+                out_copy(yh, to).start()
+
+        @pl.when(k == 7)
         def _():
             krin[part] = kro[part]
 
-        @pl.when(k == 2)
+        @pl.when(k == 5)
         def _():
             half_out(far, 0)
 
-        @pl.when(k == 0)
+        @pl.when(k == 1)
         def _():
             mixed_out.wait()
             mixf = w["mixf"]
@@ -472,11 +474,6 @@
             mixed.start()
             w["recvm"][slot] = w["stagem"][slot]
 
-    half_out(y_lo, 1)
-    mixed.finish()
-    gws = w["gws"]
-    gws[:, 32:40, :] = dot(w["recvm"][...].reshape(256, 512), w["up"][...], NT).reshape(16, 16, 128)[:, 0:8]
-
     @pl.loop(1, 8)
     def _(s):
         for y in range(2):
@@ -491,9 +488,15 @@
     backs = over(8, HEADS, slot_peer, lambda s: stage3.at[slot_at(s)], recv3.at[slot])
     backs.start()
     recv3[slot] = stage3[slot]
-
+    half_out(y_lo, 1)
+    mixed.finish()
+    gws = w["gws"]
+    gws[:, 32:40, :] = dot(w["recvm"][...].reshape(256, 512), w["up"][...], NT).reshape(16, 16, 128)[:, 0:8]
+
+    spans = (pl.ds(0, 16), pl.ds(16, 24))
+    sums = [over(5 + 4 * n, HEADS, head_peer, lambda s, c=c: gws.at[head_at(s), c], w["gwin"].at[me, c]) for n, c in enumerate(spans)]
     image = None
-    for n in (1, 0):
+    for n in (0, 1):
         if n:
             halves[0].finish()
             halves[1].finish()
@@ -502,17 +505,17 @@
             backs.finish()
             every = recv3[...].reshape(256, 512)
         gws[:, 16 * n:16 * n + 16, :] = dot(every, w["xp"][...], NT).reshape(16, 16, 128)
+        sums[n].start()
         term = dot(wall[:, 16 * n:16 * n + 16, :].reshape(256, 128), every, TN)
         image = term if image is None else image + term
-    sums = over(5, HEADS, head_peer, lambda s: gws.at[head_at(s)], w["gwin"].at[me])
-    sums.start()
     w["gwin"][me] = gws[me]
     image = image.reshape(16, 8, 512)
     w["stage4"][...] = jnp.concatenate([image[:, :, 0:256], image[:, :, 256:512]], axis=1).astype(BF16)
     images = over(6, HEADS, head_peer, lambda s: w["stage4"].at[head_at(s)], w["recv4"].at[me])
     images.start()
     w["recv4"][me] = w["stage4"][me]
-    sums.finish()
+    for trade in sums:
+        trade.finish()
     total = w["gwin"][0]
     for p in range(1, HEADS):
         total = total + w["gwin"][p]
@@ -532,7 +535,7 @@
     for p in range(1, ROWS):
         total = total + w["gwrow"][p]
     gw[...] = total * (1.0 / 256.0)
-    for trade in (inputs, weights, mapped, mixed, *halves, backs, sums, images, last):
+    for trade in (inputs, weights, mapped, mixed, *halves, backs, *sums, images, last):
         trade.drain()
 
     @pl.loop(0, 4)
@@ -568,7 +571,7 @@
         stagem=vmem((16, 16, 512), BF16), recvm=vmem((16, 16, 512), BF16),
         stage3=vmem((16, 16, 512), BF16), recv3=vmem((16, 16, 512), BF16), stageq=vmem((2, 16, 16, 256), BF16), recvq=vmem((2, 16, 16, 256), BF16), stage4=vmem((16, 16, 256), BF16), recv4=vmem((16, 16, 256), BF16),
         gws=vmem((16, 40, 128), F32), gwin=vmem((16, 40, 128), F32), part=vmem((40, 128), F32), gwrow=vmem((8, 40, 128), F32),
-        os=dma((2, 2, 8)), hs=dma((18, 16)), rs=dma((4, 8)), ps=dma((2, 21)), ks=dma((2, 4, 8)),
+        os=dma((2, 2, 8)), hs=dma((20, 16)), rs=dma((4, 8)), ps=dma((2, 21)), ks=dma((2, 4, 8)),
     )
 
 

time: 120 us -> 120 us (level)
  no operation moved by 1% of the time
where the time goes in v6:
time: 120 us
  Pallas kernels  118 us (98%)
  between operations  1.29 us (1%)
    pallas_call x1, Pallas kernels, local(): pl.pallas_call(functools.partial(layer, list(names)), out_shape=[jax.Shap...  117 us

profile of v6, /device:TPU:1, one launch (start us, length us, event | category | flops | bytes accessed | tf_op | source)
XLA Modules:
  0.0 119.5 jit_solution(6530189651505950594)
XLA Ops:
  1.3 116.7 %layer.1 = (bf16[8,32,256]{2,1,0:T(8,128)(2,1)}, f32[40,128]{1,0:T(8,128)}) custom-call(bf16[8,32,256]{2,1,0:T(8,128)(2,1)} %x.1, bf16[8,32,256]{2,1,0:T(8,128)(2,1)} %u.1, bf16[8,128]{1,0:T(8,128)(2,1)} %bitcast.8, bf16[8,128]{1,0:T(8,128)(2,1)} %bitcast.9, bf16[8,128]{1,0:T(8,128)(2,1)} %bitcast.10, bf16[8,128]{1,0:T(8,128)(2,1)} %bitcast.11, ...), custom_call_target="tpu_custom_call" | custom-call | tf_op jit(solution)/shard_map/layer/pallas_call | solution.py:581
  118.0 1.6 %results.1 = (bf16[8,32,256]{2,1,0:T(8,128)(2,1)}, f32[8,128]{1,0:T(8,128)}, f32[8,128]{1,0:T(8,128)}, f32[8,128]{1,0:T(8,128)}, f32[8,128]{1,0:T(8,128)}, /*index=5*/f32[8,128]{1,0:T(8,128)}) custom-call(bf16[8,32,256]{2,1,0:T(8,128)(2,1)} %get-tuple-element.14.grads, f32[40,128]{1,0:T(8,128)} %get-tuple-element.15.gw), custom_call_target="tpu_custom_call" | custom-call | tf_op jit(solution)/shard_map/results/pallas_call | solution.py:589

commit v7 on v6

--- a/solution.py
+++ b/solution.py
@@ -274,24 +274,24 @@
         return lax.rem(me + s, HEADS)
 
     greet([(HEADS, head_peer), (ROWS, row_peer), (HEADS, slot_peer), (8, part_peer)])
-    wself, wall, wide = w["wself"], w["wall"], w["wide"]
+    wall, wide, stage1, recv1 = w["wall"], w["wide"], w["stage1"], w["recv1"]
     f0 = jnp.full((8, 128), fac[0], F32)
     f1 = f0 - f0.astype(BF16).astype(F32)
     f2 = f1 - f1.astype(BF16).astype(F32)
     tile = lax.broadcasted_iota(jnp.int32, (8, 128), 0)
     factor = jnp.where(tile == 0, f0, jnp.where(tile == 1, f1, jnp.where(tile == 2, f2, 0.0)))
-    wself[...] = jnp.concatenate([wk[...], wr[...], wq[...], wl[...], wf[...], factor.astype(BF16)], axis=0)
+    pairs = ((wk[...], wr[...]), (wq[...], wl[...]), (wf[...], factor.astype(BF16)))
+    weights = jnp.concatenate([jnp.concatenate(pair, axis=0) for pair in pairs], axis=1)
+    for p in range(HEADS):
+        stage1[p, :, 512:896] = weights
     for z in range(2):
         wide[z, 0:256, :] = x[:, :, z * 128:z * 128 + 128].reshape(256, 128).astype(F32)
         wide[z, 256:512, :] = u[:, :, z * 128:z * 128 + 128].reshape(256, 128).astype(F32)
-    to_pairs(wide, w["stage1"], 16, 16)
+    to_pairs(wide, stage1, 16, 16)
     pl.semaphore_wait(pltpu.get_barrier_semaphore(), 2 * HEADS + ROWS + 8 - 4)
-    inputs = over(0, HEADS, head_peer, lambda s: w["stage1"].at[head_at(s)], w["recv1"].at[me])
-    weights = over(1, HEADS, head_peer, lambda s: wself, wall.at[me])
-    weights.start()
+    inputs = over(0, HEADS, head_peer, lambda s: stage1.at[head_at(s)], recv1.at[me])
     inputs.start()
-    w["recv1"][me] = w["stage1"][me]
-    wall[me] = wself[...]
+    recv1[me] = stage1[me]
     constants(w)
     node = row * 32 + lax.broadcasted_iota(jnp.int32, (32, 128), 0)
     column = lax.broadcasted_iota(jnp.int32, (32, 128), 1)
@@ -301,10 +301,11 @@
     bias = jnp.concatenate([w["mask"][z, pl.ds(2 * me + a, 1), :] for z in range(2) for a in range(2)], axis=1)
     bias = jnp.broadcast_to(bias, (8, 512))
     inputs.finish()
-    both = w["recv1"][...].astype(F32)
+    for n in range(3):
+        wall[:, 16 * n:16 * n + 16, :] = recv1[:, :, 512 + 128 * n:640 + 128 * n]
+    both = recv1[:, :, 0:512].astype(F32)
     w["xp"][...] = both[:, 0:8].reshape(128, 512).astype(BF16)
     w["up"][...] = both[:, 8:16].reshape(128, 512).astype(BF16)
-    weights.finish()
 
     stage2, recv2, kr = w["stage2"], w["recv2"], w["kr"]
     mapped = over(2, HEADS, slot_peer, lambda s: stage2.at[slot_at(s)], recv2.at[slot])
@@ -535,7 +536,7 @@
     for p in range(1, ROWS):
         total = total + w["gwrow"][p]
     gw[...] = total * (1.0 / 256.0)
-    for trade in (inputs, weights, mapped, mixed, *halves, backs, *sums, images, last):
+    for trade in (inputs, mapped, mixed, *halves, backs, *sums, images, last):
         trade.drain()
 
     @pl.loop(0, 4)
@@ -562,8 +563,8 @@
     vmem, dma = pltpu.VMEM, pltpu.SemaphoreType.DMA
     return dict(
         core_scratch(),
-        wide=vmem((2, 1024, 128), F32), wide2=vmem((2, 2048, 128), F32), wself=vmem((48, 128), BF16), wall=vmem((16, 48, 128), BF16),
-        stage1=vmem((16, 16, 512), BF16), recv1=vmem((16, 16, 512), BF16), xp=vmem((128, 512), BF16), up=vmem((128, 512), BF16),
+        wide=vmem((2, 1024, 128), F32), wide2=vmem((2, 2048, 128), F32), wall=vmem((16, 48, 128), BF16),
+        stage1=vmem((16, 16, 896), BF16), recv1=vmem((16, 16, 896), BF16), xp=vmem((128, 512), BF16), up=vmem((128, 512), BF16),
         stage2=vmem((16, 48, 512), BF16), recv2=vmem((16, 48, 512), BF16), near=vmem((16, 32, 512), BF16), mask=vmem((2, 32, 128), F32),
         kr=vmem((8, 16, 16, 256), BF16),
         ql2=vmem((2, 64, 2048), F32), qlin=vmem((2, 32, 2048), F32), kro=vmem((8, 32, 16, 128), F32), krin=vmem((8, 32, 16, 128), F32),

time: 120 us -> 119 us (level)
  no operation moved by 1% of the time
where the time goes in v7:
time: 119 us
  Pallas kernels  118 us (99%)
  between operations  1.29 us (1%)
    pallas_call x1, Pallas kernels, local(): pl.pallas_call(functools.partial(layer, list(names)), out_shape=[jax.Shap...  116 us

profile of v7, /device:TPU:1, one launch (start us, length us, event | category | flops | bytes accessed | tf_op | source)
XLA Modules:
  0.0 118.9 jit_solution(16358022535463077911)
XLA Ops:
  1.3 116.1 %layer.1 = (bf16[8,32,256]{2,1,0:T(8,128)(2,1)}, f32[40,128]{1,0:T(8,128)}) custom-call(bf16[8,32,256]{2,1,0:T(8,128)(2,1)} %x.1, bf16[8,32,256]{2,1,0:T(8,128)(2,1)} %u.1, bf16[8,128]{1,0:T(8,128)(2,1)} %bitcast.8, bf16[8,128]{1,0:T(8,128)(2,1)} %bitcast.9, bf16[8,128]{1,0:T(8,128)(2,1)} %bitcast.10, bf16[8,128]{1,0:T(8,128)(2,1)} %bitcast.11, ...), custom_call_target="tpu_custom_call" | custom-call | tf_op jit(solution)/shard_map/layer/pallas_call | solution.py:582
  117.4 1.6 %results.1 = (bf16[8,32,256]{2,1,0:T(8,128)(2,1)}, f32[8,128]{1,0:T(8,128)}, f32[8,128]{1,0:T(8,128)}, f32[8,128]{1,0:T(8,128)}, f32[8,128]{1,0:T(8,128)}, /*index=5*/f32[8,128]{1,0:T(8,128)}) custom-call(bf16[8,32,256]{2,1,0:T(8,128)(2,1)} %get-tuple-element.14.grads, f32[40,128]{1,0:T(8,128)} %get-tuple-element.15.gw), custom_call_target="tpu_custom_call" | custom-call | tf_op jit(solution)/shard_map/results/pallas_call | solution.py:590

commit v8 on v7

--- a/solution.py
+++ b/solution.py
@@ -321,6 +321,8 @@
             else:
                 recv2[slot] = stage2[slot]
 
+    for n in range(2):
+        w["turned"][n] = wall[:, 16 * n:16 * n + 16, :].reshape(256, 128).astype(F32).T.astype(BF16)
     near, wide2 = w["near"], w["wide2"]
 
     def four(g):
@@ -507,7 +509,7 @@
             every = recv3[...].reshape(256, 512)
         gws[:, 16 * n:16 * n + 16, :] = dot(every, w["xp"][...], NT).reshape(16, 16, 128)
         sums[n].start()
-        term = dot(wall[:, 16 * n:16 * n + 16, :].reshape(256, 128), every, TN)
+        term = dot(w["turned"][n], every)
         image = term if image is None else image + term
     w["gwin"][me] = gws[me]
     image = image.reshape(16, 8, 512)
@@ -515,6 +517,22 @@
     images = over(6, HEADS, head_peer, lambda s: w["stage4"].at[head_at(s)], w["recv4"].at[me])
     images.start()
     w["recv4"][me] = w["stage4"][me]
+    for trade in (inputs, mapped, mixed, *halves, backs):
+        trade.drain()
+
+    @pl.loop(0, 4)
+    def _(g):
+        near_copy(g).wait_send()
+
+        @pl.loop(1, 8)
+        def _(s):
+            kr_copy(g, s).wait_send()
+
+    @pl.loop(1, 8)
+    def _(s):
+        for y in range(2):
+            out_copy(y, lax.rem(part + s, 8)).wait_send()
+
     for trade in sums:
         trade.finish()
     total = w["gwin"][0]
@@ -536,21 +554,8 @@
     for p in range(1, ROWS):
         total = total + w["gwrow"][p]
     gw[...] = total * (1.0 / 256.0)
-    for trade in (inputs, mapped, mixed, *halves, backs, *sums, images, last):
+    for trade in (*sums, images, last):
         trade.drain()
-
-    @pl.loop(0, 4)
-    def _(g):
-        near_copy(g).wait_send()
-
-        @pl.loop(1, 8)
-        def _(s):
-            kr_copy(g, s).wait_send()
-
-    @pl.loop(1, 8)
-    def _(s):
-        for y in range(2):
-            out_copy(y, lax.rem(part + s, 8)).wait_send()
 
 
 def results(grads, gw, out, gq, gk, gl, gr, go):
@@ -564,7 +569,7 @@
     return dict(
         core_scratch(),
         wide=vmem((2, 1024, 128), F32), wide2=vmem((2, 2048, 128), F32), wall=vmem((16, 48, 128), BF16),
-        stage1=vmem((16, 16, 896), BF16), recv1=vmem((16, 16, 896), BF16), xp=vmem((128, 512), BF16), up=vmem((128, 512), BF16),
+        stage1=vmem((16, 16, 896), BF16), recv1=vmem((16, 16, 896), BF16), turned=vmem((2, 128, 256), BF16), xp=vmem((128, 512), BF16), up=vmem((128, 512), BF16),
         stage2=vmem((16, 48, 512), BF16), recv2=vmem((16, 48, 512), BF16), near=vmem((16, 32, 512), BF16), mask=vmem((2, 32, 128), F32),
         kr=vmem((8, 16, 16, 256), BF16),
         ql2=vmem((2, 64, 2048), F32), qlin=vmem((2, 32, 2048), F32), kro=vmem((8, 32, 16, 128), F32), krin=vmem((8, 32, 16, 128), F32),

time: 119 us -> 118 us (level)
  no operation moved by 1% of the time
where the time goes in v8:
time: 118 us
  Pallas kernels  117 us (99%)
  between operations  1.29 us (1%)
    pallas_call x1, Pallas kernels, local(): pl.pallas_call(functools.partial(layer, list(names)), out_shape=[jax.Shap...  115 us

profile of v8, /device:TPU:1, one launch (start us, length us, event | category | flops | bytes accessed | tf_op | source)
XLA Modules:
  0.0 117.9 jit_solution(13177611968742504868)
XLA Ops:
  1.3 115.1 %layer.1 = (bf16[8,32,256]{2,1,0:T(8,128)(2,1)}, f32[40,128]{1,0:T(8,128)}) custom-call(bf16[8,32,256]{2,1,0:T(8,128)(2,1)} %x.1, bf16[8,32,256]{2,1,0:T(8,128)(2,1)} %u.1, bf16[8,128]{1,0:T(8,128)(2,1)} %bitcast.8, bf16[8,128]{1,0:T(8,128)(2,1)} %bitcast.9, bf16[8,128]{1,0:T(8,128)(2,1)} %bitcast.10, bf16[8,128]{1,0:T(8,128)(2,1)} %bitcast.11, ...), custom_call_target="tpu_custom_call" | custom-call | tf_op jit(solution)/shard_map/layer/pallas_call | solution.py:587
  116.3 1.6 %results.1 = (bf16[8,32,256]{2,1,0:T(8,128)(2,1)}, f32[8,128]{1,0:T(8,128)}, f32[8,128]{1,0:T(8,128)}, f32[8,128]{1,0:T(8,128)}, f32[8,128]{1,0:T(8,128)}, /*index=5*/f32[8,128]{1,0:T(8,128)}) custom-call(bf16[8,32,256]{2,1,0:T(8,128)(2,1)} %get-tuple-element.14.grads, f32[40,128]{1,0:T(8,128)} %get-tuple-element.15.gw), custom_call_target="tpu_custom_call" | custom-call | tf_op jit(solution)/shard_map/results/pallas_call | solution.py:595
